TPU v7x, 32 devices: a whole 2x2x4 slice. The times are simulated.
32 devices in a mesh: gx: 4 (over z), gy: 8 (over y, x, core).
Axes of the slice: x: 2, y: 2, z: 4, core: 2. Of those that a mesh axis runs over, the one named last changes fastest.
Arguments:
- dynamics: float32 [3, 93, 8, 1024], P(None, None, 'gx', 'gy'), may hold values from -4 to 4
- tracers: float32 [33, 93, 8, 1024], P(None, None, 'gx', 'gy'), may hold values from 0.05 to 16
- thickness: float32 [93, 8, 1024], P(None, 'gx', 'gy'), may hold values from 0.005376344 to 0.017204301
- area_weight: float32 [8, 1024], P('gx', 'gy'), may hold values from 0.3 to 3
- cloud_frac: float32 [93, 8192], P(None, ('gx', 'gy')), may hold values from 0.05 to 1
- owner: int32 [8, 1024], P('gx', 'gy'), may hold values from 0 to 31, as said below
- warm_mask: int32 [8, 1024], P('gx', 'gy'), may hold values 0 or 1
Outputs:
- dynamics_new: float32 [3, 93, 8, 1024], P(None, None, 'gx', 'gy')
- tracers_new: float32 [33, 93, 8, 1024], P(None, None, 'gx', 'gy')
- increment_stack: float32 [4, 93, 8, 1024], P(None, None, 'gx', 'gy')
- cloud_next: float32 [93, 8192], P(None, ('gx', 'gy'))
Inputs may be any that keep to these rules, and one draw needn't show every extreme that they name: Every device along gx+gy owns exactly 256 columns; the columns of one device that go to one owner number at most 16.
All inputs are finite; a program needn't handle non-finite values. No bound on the sum of `warm_mask` on one device may be relied on, other than what follows from the above.
Results may differ from a plain program's by a relative error of at most 0.0003.
Values sent between devices are 32-bit elements; how exact they have to be, the bound alone decides.
No kernel may reach another device: no remote copies, remote signals or barrier semaphores. Data moves between devices by JAX's collectives and lax.ppermute only.
A program may use at most 128 MiB of HBM per device.

v0:
```python
import jax
import jax.numpy as jnp
from jax import lax
from jax.sharding import PartitionSpec as P

NP = 4


top_pressure = 0.002
mid_pressure = 0.6
kappa_sat = 0.06
phase_change_warming = 0.25
auto_rate = 0.8
accrete_rate = 0.5
fall_rate = 20.0
edges_per_block = 16


def with_halo(shard, sides, width):
    for axis, dim in sides:
        size, length = (lax.axis_size(axis), shard.shape[dim])
        up = [(i, (i + 1) % size) for i in range(size)]
        down = [(j, i) for i, j in up]
        last = lax.slice_in_dim(shard, length - width, length, axis=dim)
        leading = lax.slice_in_dim(shard, 0, width, axis=dim)
        before = lax.ppermute(last, axis, up)
        after = lax.ppermute(leading, axis, down)
        shard = jnp.concatenate([before, shard, after], axis=dim)
    return shard


def target_edges(ground_deposit_rate, number_of_layers_total):
    sigma = (
        jnp.arange(number_of_layers_total + 1).astype(ground_deposit_rate.dtype)
        / number_of_layers_total
    )[:, None]
    return (
        top_pressure * (1.0 - sigma)
        + sigma * sigma * ground_deposit_rate[None, :]
        + sigma * (1.0 - sigma) * mid_pressure
    )


def remap_columns(fields, thick):
    number_of_layers_total = thick.shape[0]
    columns = thick.shape[1]
    nfields = fields.shape[0]
    source = jnp.concatenate(
        [
            jnp.full((1, columns), top_pressure, thick.dtype),
            top_pressure + jnp.cumsum(thick, axis=0),
        ],
        0,
    )
    ground_deposit_rate = source[-1]
    target = target_edges(ground_deposit_rate, number_of_layers_total)
    thick_tgt = target[1:] - target[:-1]
    below = jnp.concatenate([fields[:, :1], fields[:, :-1]], 1)
    above = jnp.concatenate([fields[:, 1:], fields[:, -1:]], 1)
    above_two = jnp.concatenate([fields[:, 2:], fields[:, -1:], fields[:, -1:]], 1)
    edge = 7.0 / 12.0 * (fields + above) - 1.0 / 12.0 * (below + above_two)
    edge = jnp.clip(edge, jnp.minimum(fields, above), jnp.maximum(fields, above))
    left = jnp.concatenate([fields[:, :1], edge[:, :-1]], 1)
    sixth = 6.0 * fields - 3.0 * (left + edge)
    coeffs = jnp.stack([left, edge - left + sixth, -sixth]) * thick[None, None]
    edge_count = number_of_layers_total + 1
    block_count = -(-edge_count // edges_per_block)
    padded_target = jnp.pad(
        target, ((0, block_count * edges_per_block - edge_count), (0, 0)), mode="edge"
    )
    target_blocks = padded_target.reshape(block_count, edges_per_block, columns)
    source_top = source[:-1]

    def one_block(rows):
        frac = jnp.clip((rows[:, None, :] - source_top[None, :, :]) / thick[None], 0.0, 1.0)
        powers = jnp.stack([frac, frac * frac * 0.5, frac * frac * frac / 3.0])
        return jnp.einsum("jtkc,jfkc->tfc", powers, coeffs, precision=lax.Precision.HIGHEST)

    cumulative = lax.map(one_block, target_blocks).reshape(
        block_count * edges_per_block, nfields, columns
    )[:edge_count]
    remapped = jnp.transpose((cumulative[1:] - cumulative[:-1]) / thick_tgt[:, None, :], (1, 0, 2))
    return (remapped, ground_deposit_rate)


def vertical_profile_microscale(
    ambient_kelvin_state,
    moisture_mixratio,
    droplet_mixratio,
    falling_drops_mixratio,
    ground_deposit_rate,
    present_droplet_mixratio,
    above_freezing_marker,
):
    number_of_layers_total = ambient_kelvin_state.shape[0]
    edges = target_edges(ground_deposit_rate, number_of_layers_total)
    layer = edges[1:] - edges[:-1]
    middle = 0.5 * (edges[1:] + edges[:-1])
    centigrade_reading = 10.0 * ambient_kelvin_state
    saturation = 3.8 / middle * jnp.exp(17.27 * centigrade_reading / (centigrade_reading + 237.3))
    phase_change_mass = jnp.maximum(
        (moisture_mixratio - saturation) / (1.0 + kappa_sat * saturation), -droplet_mixratio
    )
    revised_moisture_mixratio = moisture_mixratio - phase_change_mass
    liquid_mid = droplet_mixratio + phase_change_mass
    revised_kelvin_state = ambient_kelvin_state + phase_change_warming * phase_change_mass
    converted = liquid_mid * (
        1.0
        - jnp.exp(-(auto_rate * present_droplet_mixratio + accrete_rate * falling_drops_mixratio))
    )
    warm = (above_freezing_marker == 1)[None, :]
    revised_droplet_mixratio = jnp.where(warm, liquid_mid - converted, liquid_mid)
    rain_mid = jnp.where(warm, falling_drops_mixratio + converted, falling_drops_mixratio)
    falling = fall_rate * (0.5 + present_droplet_mixratio)

    def descend(outflow, inputs):
        amount, speed = inputs
        kept = (amount + outflow) / (1.0 + speed)
        return (speed * kept, kept)

    outflow_end, settled = lax.scan(
        descend, jnp.zeros_like(ground_deposit_rate), (rain_mid * layer, falling)
    )
    revised_drops_mixratio = jnp.where(warm, settled / layer, rain_mid)
    target = jnp.clip((revised_moisture_mixratio / saturation - 0.7) / 0.3, 0.05, 1.0)
    cloud_new = present_droplet_mixratio + 0.5 * (target - present_droplet_mixratio)
    increment_stack = jnp.stack(
        [
            revised_kelvin_state - ambient_kelvin_state,
            revised_moisture_mixratio - moisture_mixratio,
            revised_droplet_mixratio - droplet_mixratio,
            revised_drops_mixratio - falling_drops_mixratio,
        ]
    )
    return (increment_stack, cloud_new)


def fold_edges(padded, dim, period):
    count = padded.shape[dim] - 2
    inner = lax.slice_in_dim(padded, 1, count + 1, axis=dim)
    before = lax.slice_in_dim(padded, 0, count, axis=dim)
    after = lax.slice_in_dim(padded, 2, count + 2, axis=dim)
    phase = lax.broadcasted_iota(jnp.int32, inner.shape, dim) % period
    return inner + jnp.where(phase == 0, before, 0.0) + jnp.where(phase == period - 1, after, 0.0)


def local(dynamics, tracers, thickness, area_weight, cloud_frac, owner, warm_mask):
    number_of_layers_total = thickness.shape[0]
    rows_here = thickness.shape[1]
    cols_here = thickness.shape[2]
    columns = rows_here * cols_here
    ndyn = dynamics.shape[0]
    nfields = ndyn + tracers.shape[0]
    weight = area_weight[None] * thickness
    stacked = jnp.concatenate(
        [
            weight[None] * dynamics,
            weight[None] * tracers,
            weight[None],
            jnp.broadcast_to(area_weight, weight.shape)[None],
        ],
        0,
    )
    padded_rows = with_halo(stacked, (("gx", 2),), 1)
    partial_sum = fold_edges(padded_rows, 2, rows_here)
    padded_cols = with_halo(partial_sum, (("gy", 3),), 1)
    summed = fold_edges(padded_cols, 3, NP)
    mass = summed[nfields]
    thick_new = mass / summed[nfields + 1]
    fields_new = summed[:nfields] / mass[None]
    remapped, ground_deposit_rate = remap_columns(
        fields_new.reshape(nfields, number_of_layers_total, columns),
        thick_new.reshape(number_of_layers_total, columns),
    )
    devices = lax.axis_size(("gx", "gy"))
    capacity = 2 * columns // devices
    slots_all = devices * capacity
    owner_cols = owner.reshape(columns)
    warm_cols = warm_mask.reshape(columns)
    onehot = (owner_cols[:, None] == jnp.arange(devices, dtype=jnp.int32)[None, :]).astype(
        jnp.int32
    )
    earlier = jnp.cumsum(onehot, axis=0) - onehot
    rank_cols = jnp.sum(earlier * onehot, axis=1)
    position = owner_cols * capacity + rank_cols
    sources = (
        jnp.zeros((slots_all,), jnp.int32).at[position].set(jnp.arange(columns, dtype=jnp.int32))
    )
    occupied = jnp.zeros((slots_all,), jnp.int32).at[position].set(1)
    payload = jnp.stack(
        [remapped[0], remapped[ndyn], remapped[ndyn + 1], remapped[ndyn + 2]]
    ).reshape(4 * number_of_layers_total, columns)
    live = occupied[None, :] == 1
    outgoing = jnp.where(live, jnp.take(payload, sources, axis=1), 0.0)
    out_surface = jnp.where(live, ground_deposit_rate[sources][None, :], 1.0)
    out_warm = (warm_cols[sources] * occupied)[None, :]
    arrived_cols, arrived_surface, arrived_warm, arrived_flags = (
        lax.all_to_all(outgoing, ("gx", "gy"), split_axis=1, concat_axis=1, tiled=True),
        lax.all_to_all(out_surface, ("gx", "gy"), split_axis=1, concat_axis=1, tiled=True),
        lax.all_to_all(out_warm, ("gx", "gy"), split_axis=1, concat_axis=1, tiled=True),
        lax.all_to_all(occupied[None, :], ("gx", "gy"), split_axis=1, concat_axis=1, tiled=True),
    )
    arrived = arrived_flags[0]
    slot = jnp.cumsum(arrived) - arrived
    target_slot = jnp.where(arrived == 1, slot, columns)
    picks = (
        jnp.zeros((columns,), jnp.int32)
        .at[target_slot]
        .set(jnp.arange(slots_all, dtype=jnp.int32), mode="drop")
    )
    slot, picks = (jnp.minimum(slot, columns - 1), picks)
    group = jnp.take(arrived_cols, picks, axis=1).reshape(4, number_of_layers_total, columns)
    group_tend, cloud_next = vertical_profile_microscale(
        group[0],
        group[1],
        group[2],
        group[3],
        arrived_surface[0][picks],
        cloud_frac,
        arrived_warm[0][picks],
    )
    returning = jnp.where(
        arrived_flags == 1,
        jnp.take(group_tend.reshape(4 * number_of_layers_total, columns), slot, axis=1),
        0.0,
    )
    back = lax.all_to_all(returning, ("gx", "gy"), split_axis=1, concat_axis=1, tiled=True)
    tend_cols = jnp.take(back, position, axis=1).reshape(4, number_of_layers_total, columns)
    dynamics_new = remapped[:ndyn].reshape(ndyn, number_of_layers_total, rows_here, cols_here)
    tracers_new = remapped[ndyn:].reshape(
        nfields - ndyn, number_of_layers_total, rows_here, cols_here
    )
    increment_stack = tend_cols.reshape(4, number_of_layers_total, rows_here, cols_here)
    return (dynamics_new, tracers_new, increment_stack, cloud_next)


def solution(mesh):
    placed = (
        P(None, None, "gx", "gy"),
        P(None, None, "gx", "gy"),
        P(None, "gx", "gy"),
        P("gx", "gy"),
        P(None, ("gx", "gy")),
        P("gx", "gy"),
        P("gx", "gy"),
    )
    return jax.shard_map(
        local,
        mesh=mesh,
        in_specs=placed,
        out_specs=(
            P(None, None, "gx", "gy"),
            P(None, None, "gx", "gy"),
            P(None, None, "gx", "gy"),
            P(None, ("gx", "gy")),
        ),
        check_vma=False,
    )
```

profile of v0, /device:TPU:0, one launch (start us, length us, event | category | flops | bytes accessed | tf_op | source)
XLA Modules:
  0.0 482.4 jit_solution(12073599962857948405)
XLA Ops:
  7.4 4.6 fusion.50
  24.1 4.3 all-to-all-start
  36.8 4.8 gather_fusion.2
  43.0 54.7 %all-to-all-done = s32[1,32,16]{2,0,1:T(1,128)S(1)} async-done(((s32[1,32,16]{2,0,1:T(1,128)}), s32[1,32,16]{2,0,1:T(1,128)S(1)}, u32[]{:S(2)}, u32[]{:S(2)}) %all-to-all-start) | async-done | bytes 2080 | tf_op jit(solution)/shard_map/all_to_all | solution.py:201
  109.4 31.4 %fusion.13 = f32[38,93,2,128]{3,2,1,0:T(2,128)S(1)} fusion(f32[38,93,1,128]{3,2,1,0:T(1,128)} %collective-permute-done.1, f32[1,93,2,128]{3,2,1,0:T(2,128)} %copy-done.7, f32[1,93,2,128]{3,2,1,0:T(2,128)S(1)} %fusion.53, f32[33,93,2,128]{3,2,1,0:T(2,128)S(1)} %broadcast_multiply_fusion, f32[3,93,2,128]{3,2,1,0:T(2,128)S(1)} %broadcast_multiply_fusion.1, ...), kind=kLoop, calls=%fused_computation.41 | loop fusion | flops 16284672 | bytes 10856466 | tf_op jit(solution)/shard_map/add | solution.py:144
  140.8 6.9 %fusion.49 = (f32[38,93,2,1]{3,2,1,0:T(2,128)}, f32[38,93,2,1]{3,2,1,0:T(2,128)}) fusion(f32[38,93,2,128]{3,2,1,0:T(2,128)S(1)} %fusion.13), kind=kLoop, calls=%fused_computation.166 | loop fusion | bytes 113088 | tf_op jit(solution)/shard_map/slice | solution.py:24
  147.7 4.2 copy.191
  152.0 4.2 copy.193
  166.9 14.1 %fusion.15 = f32[38,93,2,128]{3,2,1,0:T(2,128)S(1)} fusion(f32[38,93,2,128]{3,2,1,0:T(2,128)} %copy-done.2, f32[38,93,2,1]{3,2,1,0:T(2,128)} %copy.194, f32[38,93,2,1]{3,2,1,0:T(2,128)} %copy.192, pred[128]{0:T(512)(128)(4,1)S(1)} %copy-done.29, s32[128]{0:T(128)S(1)} %copy-done.30, s32[128]{0:T(128)S(1)} %copy-done.31), kind=kLoop, calls=%fused_computation.43 | loop fusion | flops 8142336 | bytes 7295328 | tf_op jit(solution)/shard_map/add | solution.py:144
  185.8 4.4 reshape.585
  191.0 6.3 %slice_bitcast_fusion.5 = (f32[1,36,92,256]{3,2,1,0:T(8,128)}, f32[1,36,92,256]{3,2,1,0:T(8,128)}, f32[36,92,256]{2,1,0:T(8,128)}, f32[36,92,256]{2,1,0:T(8,128)}) fusion(f32[36,93,256]{2,1,0:T(8,128)S(1)} %reshape.585), kind=kLoop, calls=%fused_computation.164 | loop fusion | bytes 20348928 | tf_op jit(solution)/shard_map/concatenate | solution.py:59
  197.3 4.1 slice_bitcast_fusion.4
  201.3 5.6 %reshape.586 = f32[1,36,93,256]{3,2,1,0:T(8,128)} reshape(f32[36,93,2,128]{3,2,1,0:T(2,128)} %slice_divide_fusion) | data formatting | bytes 6856704 | tf_op jit(solution)/shard_map/reshape | solution.py:172
  208.6 6.1 %fusion.25 = f32[36,92,256]{2,1,0:T(8,128)S(1)} fusion(f32[36,1,256]{2,1,0:T(1,128)} %get-tuple-element.233, f32[36,92,256]{2,1,0:T(8,128)} %get-tuple-element.227, f32[36,1,256]{2,1,0:T(1,128)} %get-tuple-element.234, f32[36,91,256]{2,1,0:T(8,128)} %get-tuple-element.230, f32[36,92,256]{2,1,0:T(8,128)} %get-tuple-element.228), kind=kLoop, calls=%fused_computation.64 | loop fusion | flops 11022336 | bytes 13602816 | tf_op jit(solution)/shard_map/jit(clip)/min | solution.py:62
  220.8 4.7 gather_fusion
  231.5 6.7 %subtract_add_fusion = (f32[1,36,93,256]{3,2,1,0:T(8,128)S(1)}, f32[1,36,93,256]{3,2,1,0:T(8,128)S(1)}) fusion(f32[1,36,92,256]{3,2,1,0:T(8,128)S(1)} %bitcast.132, f32[1,36,1,256]{3,2,1,0:T(1,128)} %get-tuple-element.232, f32[1,36,93,256]{3,2,1,0:T(8,128)} %reshape.586, f32[1,36,1,256]{3,2,1,0:T(1,128)} %get-tuple-element.231, ...), kind=kLoop, calls=%fused_computation.71 | loop fusion | flops 17998848 | bytes 23887872 | tf_op jit(solution)/shard_map/add | solution.py:65
  238.3 4.4 maximum_multiply_fusion
  242.7 13.7 %copy.204 = f32[3,36,93,256]{2,1,0,3:T(8,128)} copy(f32[3,36,93,256]{3,2,1,0:T(8,128)} %maximum_multiply_fusion) | data formatting | bytes 20570112 | tf_op jit(solution)/shard_map/while | solution.py:79
  256.6 6.0 %all-to-all-start.3 = ((s32[1,32,16]{2,0,1:T(1,128)}), s32[1,32,16]{2,0,1:T(1,128)S(1)}, u32[]{:S(2)}, u32[]{:S(2)}) async-start(s32[1,32,16]{2,0,1:T(1,128)} %bitcast.42), calls=%async_computation.3 | async-start | bytes 32768 | tf_op jit(solution)/shard_map/all_to_all | solution.py:200
  267.3 138.0 %while.23 = (s32[]{:T(128)}, f32[6,16,36,256]{3,1,0,2:T(8,128)}, f32[6,16,256]{2,1,0:T(8,128)S(1)}, f32[93,256]{0,1:T(8,128)S(1)}, f32[93,2,128]{0,2,1:T(8,128)S(1)}, /*index=5*/f32[3,36,93,256]{2,1,0,3:T(8,128)}, s32[]{:T(128)}) while((s32[]{:T(128)}, f32[6,16,36,256]{3,1,0,2:T(8,128)}, f32[6,16,256]{2,1,0:T(8,128)S(1)}, ...), condition=%wide.region_2.3_spmd, body=%wide.region_1.2_spmd.sunk | while | flops 498634752 | bytes 22649424 | solution.py:79
  268.1 19.9 %fusion.60 = f32[1,16,36,256]{2,1,3,0:T(8,128)S(1)} fusion(f32[3,36,93,256]{2,1,0,3:T(8,128)} %get-tuple-element.348, f32[1,16,93,256]{2,1,0,3:T(8,128)S(1)} %get-tuple-element.317, f32[1,16,93,256]{2,1,0,3:T(8,128)S(1)} %get-tuple-element.318, f32[1,16,93,256]{2,1,0,3:T(8,128)S(1)} %get-tuple-element.319), kind=kOutput, calls=%fused_computation.21.clone.1 | convolution fusion | flops 495968256 | bytes 15446016 | tf_op jit(solution)/shard_map/while/body/eval_jaxpr/jtkc,jfkc->tfc/dot_general | solution.py:77
  291.1 19.9 %fusion.60 = f32[1,16,36,256]{2,1,3,0:T(8,128)S(1)} fusion(f32[3,36,93,256]{2,1,0,3:T(8,128)} %get-tuple-element.348, f32[1,16,93,256]{2,1,0,3:T(8,128)S(1)} %get-tuple-element.317, f32[1,16,93,256]{2,1,0,3:T(8,128)S(1)} %get-tuple-element.318, f32[1,16,93,256]{2,1,0,3:T(8,128)S(1)} %get-tuple-element.319), kind=kOutput, calls=%fused_computation.21.clone.1 | convolution fusion | flops 495968256 | bytes 15446016 | tf_op jit(solution)/shard_map/while/body/eval_jaxpr/jtkc,jfkc->tfc/dot_general | solution.py:77
  314.2 19.9 %fusion.60 = f32[1,16,36,256]{2,1,3,0:T(8,128)S(1)} fusion(f32[3,36,93,256]{2,1,0,3:T(8,128)} %get-tuple-element.348, f32[1,16,93,256]{2,1,0,3:T(8,128)S(1)} %get-tuple-element.317, f32[1,16,93,256]{2,1,0,3:T(8,128)S(1)} %get-tuple-element.318, f32[1,16,93,256]{2,1,0,3:T(8,128)S(1)} %get-tuple-element.319), kind=kOutput, calls=%fused_computation.21.clone.1 | convolution fusion | flops 495968256 | bytes 15446016 | tf_op jit(solution)/shard_map/while/body/eval_jaxpr/jtkc,jfkc->tfc/dot_general | solution.py:77
  337.2 19.9 %fusion.60 = f32[1,16,36,256]{2,1,3,0:T(8,128)S(1)} fusion(f32[3,36,93,256]{2,1,0,3:T(8,128)} %get-tuple-element.348, f32[1,16,93,256]{2,1,0,3:T(8,128)S(1)} %get-tuple-element.317, f32[1,16,93,256]{2,1,0,3:T(8,128)S(1)} %get-tuple-element.318, f32[1,16,93,256]{2,1,0,3:T(8,128)S(1)} %get-tuple-element.319), kind=kOutput, calls=%fused_computation.21.clone.1 | convolution fusion | flops 495968256 | bytes 15446016 | tf_op jit(solution)/shard_map/while/body/eval_jaxpr/jtkc,jfkc->tfc/dot_general | solution.py:77
  360.2 19.9 %fusion.60 = f32[1,16,36,256]{2,1,3,0:T(8,128)S(1)} fusion(f32[3,36,93,256]{2,1,0,3:T(8,128)} %get-tuple-element.348, f32[1,16,93,256]{2,1,0,3:T(8,128)S(1)} %get-tuple-element.317, f32[1,16,93,256]{2,1,0,3:T(8,128)S(1)} %get-tuple-element.318, f32[1,16,93,256]{2,1,0,3:T(8,128)S(1)} %get-tuple-element.319), kind=kOutput, calls=%fused_computation.21.clone.1 | convolution fusion | flops 495968256 | bytes 15446016 | tf_op jit(solution)/shard_map/while/body/eval_jaxpr/jtkc,jfkc->tfc/dot_general | solution.py:77
  383.2 19.9 %fusion.60 = f32[1,16,36,256]{2,1,3,0:T(8,128)S(1)} fusion(f32[3,36,93,256]{2,1,0,3:T(8,128)} %get-tuple-element.348, f32[1,16,93,256]{2,1,0,3:T(8,128)S(1)} %get-tuple-element.317, f32[1,16,93,256]{2,1,0,3:T(8,128)S(1)} %get-tuple-element.318, f32[1,16,93,256]{2,1,0,3:T(8,128)S(1)} %get-tuple-element.319), kind=kOutput, calls=%fused_computation.21.clone.1 | convolution fusion | flops 495968256 | bytes 15446016 | tf_op jit(solution)/shard_map/while/body/eval_jaxpr/jtkc,jfkc->tfc/dot_general | solution.py:77
  413.9 6.0 %all-to-all-start.1 = ((f32[372,32,16]{0,2,1:T(8,128)}), f32[372,32,16]{0,2,1:T(8,128)S(1)}, u32[]{:S(2)}, u32[]{:S(2)}) async-start(f32[372,32,16]{0,2,1:T(8,128)} %bitcast.35), calls=%async_computation.1 | async-start | bytes 1572864 | tf_op jit(solution)/shard_map/all_to_all | solution.py:198
  422.8 17.8 %all-to-all-done.1 = f32[372,32,16]{0,2,1:T(8,128)S(1)} async-done(((f32[372,32,16]{0,2,1:T(8,128)}), f32[372,32,16]{0,2,1:T(8,128)S(1)}, u32[]{:S(2)}, u32[]{:S(2)}) %all-to-all-start.1) | async-done | bytes 761888 | tf_op jit(solution)/shard_map/all_to_all | solution.py:198
  442.4 9.6 %while.24 = (s32[]{:T(128)}, f32[256]{0:T(256)S(1)}, f32[93,256]{1,0:T(8,128)S(1)}, f32[93,256]{1,0:T(8,128)S(1)}, f32[93,256]{1,0:T(8,128)S(1)}, /*index=5*/s32[]{:T(128)}, s32[]{:T(128)}) while((s32[]{:T(128)}, f32[256]{0:T(256)S(1)}, f32[93,256]{1,0:T(8,128)S(1)}, f32[93,256]{1,0:T(8,128)S(1)}, f32[93,256]{1,0:T(8,128)S(1)}, ...), condition=%wide.region_12.15_spmd.clone, body=%wide.region_11.14_spmd.clone.sunk | while | flops 1283 | bytes 11359 | solution.py:121
  459.4 3.9 slice.214
  463.4 5.3 %reshape.589 = f32[33,93,2,128]{3,2,1,0:T(2,128)} reshape(f32[33,93,256]{2,1,0:T(8,128)} %slice.214) | data formatting | bytes 6285312 | tf_op jit(solution)/shard_map/reshape | solution.py:230
  470.2 9.8 %all-to-all-done.4 = f32[372,32,16]{0,2,1:T(8,128)S(1)} async-done(((f32[372,32,16]{0,2,1:T(8,128)}), f32[372,32,16]{0,2,1:T(8,128)S(1)}, u32[]{:S(2)}, u32[]{:S(2)}) %all-to-all-start.4) | async-done | bytes 761888 | tf_op jit(solution)/shard_map/all_to_all | solution.py:227
  (504 shorter events, 123.8 us)
Async XLA Ops:
  0.6 36.2 %copy-start = (s32[2,128]{1,0:T(2,128)S(1)}, s32[2,128]{1,0:T(2,128)}, u32[]{:S(2)}) copy-start(s32[2,128]{1,0:T(2,128)} %param.21) | copy-start | bytes 3076
  0.6 4.9 %copy-start.13 = (f32[3,93,2,128]{3,2,1,0:T(2,128)S(1)}, f32[3,93,2,128]{3,2,1,0:T(2,128)}, u32[]{:S(2)}) copy-start(f32[3,93,2,128]{3,2,1,0:T(2,128)} %param.15) | copy-start | bytes 857092
  7.4 9.7 %copy-start.16 = (s32[2,128]{1,0:T(2,128)S(1)}, s32[2,128]{1,0:T(2,128)}, u32[]{:S(2)}) copy-start(s32[2,128]{1,0:T(2,128)} %param.20) | copy-start | bytes 3076
  12.0 97.3 %collective-permute-start = (f32[38,93,1,128]{3,2,1,0:T(1,128)}, f32[38,93,1,128]{3,2,1,0:T(1,128)}, u32[]{:S(2)}, u32[]{:S(2)}) collective-permute-start(f32[38,93,1,128]{3,2,1,0:T(1,128)} %get-tuple-element.221), channel_id=1, source_target_pairs={{0,8},{8,16},{16,24},{24,0},{1,9},{9,17},{17,25},{25,1},{2,10},{10... | collective-permute-start | bytes 5428232 | tf_op jit(solution)/shard_map/ppermute | solution.py:26
  15.1 94.3 %collective-permute-start.1 = (f32[38,93,1,128]{3,2,1,0:T(1,128)}, f32[38,93,1,128]{3,2,1,0:T(1,128)}, u32[]{:S(2)}, u32[]{:S(2)}) collective-permute-start(f32[38,93,1,128]{3,2,1,0:T(1,128)} %get-tuple-element.222), channel_id=1, source_target_pairs={{8,0},{16,8},{24,16},{0,24},{9,1},{17,9},{25,17},{1,25},{10,2},{18... | collective-permute-start | bytes 5428232 | tf_op jit(solution)/shard_map/ppermute | solution.py:27
  24.1 73.6 %all-to-all-start = ((s32[1,32,16]{2,0,1:T(1,128)}), s32[1,32,16]{2,0,1:T(1,128)S(1)}, u32[]{:S(2)}, u32[]{:S(2)}) async-start(s32[1,32,16]{2,0,1:T(1,128)} %bitcast.147), calls=%async_computation | async-start | bytes 32768 | tf_op jit(solution)/shard_map/all_to_all | solution.py:201
  109.3 31.5 %copy-start.27 = (s32[256]{0:T(256)}, s32[256]{0:T(256)S(1)}, u32[]{:S(2)}) copy-start(s32[256]{0:T(256)S(1)} %scatter_custom_fusion.2) | copy-start | bytes 3076
  140.8 6.9 %copy-start.2 = (f32[38,93,2,128]{3,2,1,0:T(2,128)}, f32[38,93,2,128]{3,2,1,0:T(2,128)S(1)}, u32[]{:S(2)}) copy-start(f32[38,93,2,128]{3,2,1,0:T(2,128)S(1)} %fusion.13) | copy-start | bytes 10856452
  152.0 7.5 %collective-permute-start.2 = (f32[38,93,2,1]{1,2,3,0:T(2,128)S(1)}, f32[38,93,2,1]{1,2,3,0:T(2,128)S(1)}, u32[]{:S(2)}, u32[]{:S(2)}) collective-permute-start(f32[38,93,2,1]{1,2,3,0:T(2,128)S(1)} %copy.191), channel_id=1, source_target_pairs={{0,1},{1,2},{2,3},{3,4},{4,5},{5,6},{6,7},{7,0},{8,9},{9,10},{10,1... | collective-permute-start | bytes 84824 | tf_op jit(solution)/shard_map/ppermute | solution.py:26
  156.3 7.0 %collective-permute-start.3 = (f32[38,93,2,1]{1,2,3,0:T(2,128)S(1)}, f32[38,93,2,1]{1,2,3,0:T(2,128)S(1)}, u32[]{:S(2)}, u32[]{:S(2)}) collective-permute-start(f32[38,93,2,1]{1,2,3,0:T(2,128)S(1)} %copy.193), channel_id=1, source_target_pairs={{1,0},{2,1},{3,2},{4,3},{5,4},{6,5},{7,6},{0,7},{9,8},{10,9},{11,1... | collective-permute-start | bytes 84824 | tf_op jit(solution)/shard_map/ppermute | solution.py:27
  159.5 7.5 %copy-start.29 = (pred[128]{0:T(512)(128)(4,1)S(1)}, pred[128]{0:T(512)(128)(4,1)}, u32[]{:S(2)}) copy-start(pred[128]{0:T(512)(128)(4,1)} %compare_and_fusion.4) | copy-start | bytes 388
  159.5 7.5 %copy-start.30 = (s32[128]{0:T(128)S(1)}, s32[128]{0:T(128)}, u32[]{:S(2)}) copy-start(s32[128]{0:T(128)} %get-tuple-element.243) | copy-start | bytes 1540
  159.5 7.5 %copy-start.31 = (s32[128]{0:T(128)S(1)}, s32[128]{0:T(128)}, u32[]{:S(2)}) copy-start(s32[128]{0:T(128)} %get-tuple-element.244) | copy-start | bytes 1540
  208.6 6.1 %copy-start.12 = (f32[36,1,256]{2,1,0:T(1,128)S(1)}, f32[36,1,256]{2,1,0:T(1,128)}, u32[]{:S(2)}) copy-start(f32[36,1,256]{2,1,0:T(1,128)} %get-tuple-element.234) | copy-start | bytes 110596
  214.7 6.1 %copy-start.15 = (s32[1024]{0:T(1024)S(1)}, s32[1024]{0:T(1024)}, u32[]{:S(2)}) copy-start(s32[1024]{0:T(1024)} %pad_clamp_fusion.3) | copy-start | bytes 12292
  228.1 28.5 %all-to-all-start.2 = ((f32[1,32,16]{2,0,1:T(1,128)}), f32[1,32,16]{2,0,1:T(1,128)}, u32[]{:S(2)}, u32[]{:S(2)}) async-start(f32[1,32,16]{2,0,1:T(1,128)} %bitcast.148), calls=%async_computation.2 | async-start | bytes 32768 | tf_op jit(solution)/shard_map/all_to_all | solution.py:199
  231.5 6.7 %copy-start.5 = (f32[1,36,93,256]{3,2,1,0:T(8,128)S(1)}, f32[1,36,93,256]{3,2,1,0:T(8,128)}, u32[]{:S(2)}) copy-start(f32[1,36,93,256]{3,2,1,0:T(8,128)} %maximum_bitcast_fusion) | copy-start | bytes 10285060
  231.5 6.7 %copy-start.6 = (f32[12,8,2,128]{3,1,2,0:T(8,128)S(1)}, f32[12,8,2,128]{3,1,2,0:T(8,128)}, u32[]{:S(2)}) copy-start(f32[12,8,2,128]{3,1,2,0:T(8,128)} %copy.231) | copy-start | bytes 294916
  238.2 4.4 copy-start.9
  242.7 13.8 %copy-start.10 = (f32[93,2,128]{2,1,0:T(2,128)S(1)}, f32[93,2,128]{2,1,0:T(2,128)}, u32[]{:S(2)}) copy-start(f32[93,2,128]{2,1,0:T(2,128)} %bitcast_divide_fusion) | copy-start | bytes 285700
  242.7 23.8 %copy-start.32 = (f32[94]{0:T(128)S(1)}, f32[94]{0:T(128)}, u32[]{:S(2)}) copy-start(f32[94]{0:T(128)} %get-tuple-element.245) | copy-start | bytes 1132
  242.7 23.8 %copy-start.33 = (f32[94]{0:T(128)S(1)}, f32[94]{0:T(128)}, u32[]{:S(2)}) copy-start(f32[94]{0:T(128)} %get-tuple-element.246) | copy-start | bytes 1132
  242.7 23.8 %copy-start.34 = (f32[94]{0:T(128)S(1)}, f32[94]{0:T(128)}, u32[]{:S(2)}) copy-start(f32[94]{0:T(128)} %fusion.46) | copy-start | bytes 1132
  256.6 157.3 %all-to-all-start.3 = ((s32[1,32,16]{2,0,1:T(1,128)}), s32[1,32,16]{2,0,1:T(1,128)S(1)}, u32[]{:S(2)}, u32[]{:S(2)}) async-start(s32[1,32,16]{2,0,1:T(1,128)} %bitcast.42), calls=%async_computation.3 | async-start | bytes 32768 | tf_op jit(solution)/shard_map/all_to_all | solution.py:200
  411.1 8.8 %copy-start.14 = (f32[93,256]{1,0:T(8,128)S(1)}, f32[93,256]{1,0:T(8,128)}, u32[]{:S(2)}) copy-start(f32[93,256]{1,0:T(8,128)} %param.19) | copy-start | bytes 285700
  412.8 10.0 %copy-start.21 = (s32[512]{0:T(512)S(1)}, s32[512]{0:T(512)}, u32[]{:S(2)}) copy-start(s32[512]{0:T(512)} %get-tuple-element.204) | copy-start | bytes 6148
  412.8 10.0 %copy-start.28 = (s32[256]{0:T(256)S(1)}, s32[256]{0:T(256)}, u32[]{:S(2)}) copy-start(s32[256]{0:T(256)} %copy-done.27) | copy-start | bytes 3076
  413.9 26.7 %all-to-all-start.1 = ((f32[372,32,16]{0,2,1:T(8,128)}), f32[372,32,16]{0,2,1:T(8,128)S(1)}, u32[]{:S(2)}, u32[]{:S(2)}) async-start(f32[372,32,16]{0,2,1:T(8,128)} %bitcast.35), calls=%async_computation.1 | async-start | bytes 1572864 | tf_op jit(solution)/shard_map/all_to_all | solution.py:198
  453.0 6.4 %copy-start.17 = (s32[2,128]{1,0:T(2,128)S(1)}, s32[2,128]{1,0:T(2,128)}, u32[]{:S(2)}) copy-start(s32[2,128]{1,0:T(2,128)} %param.20) | copy-start | bytes 3076
  453.0 6.4 %copy-start.20 = (s32[256]{0:T(256)S(1)}, s32[256]{0:T(256)}, u32[]{:S(2)}) copy-start(s32[256]{0:T(256)} %copy-done.19) | copy-start | bytes 3076
  455.7 24.3 %all-to-all-start.4 = ((f32[372,32,16]{0,2,1:T(8,128)}), f32[372,32,16]{0,2,1:T(8,128)S(1)}, u32[]{:S(2)}, u32[]{:S(2)}) async-start(f32[372,32,16]{0,2,1:T(8,128)} %bitcast.46), calls=%async_computation.4 | async-start | bytes 1572864 | tf_op jit(solution)/shard_map/all_to_all | solution.py:227
  463.4 18.8 %copy-start.1 = (s32[2,128]{1,0:T(2,128)S(1)}, s32[2,128]{1,0:T(2,128)}, u32[]{:S(2)}) copy-start(s32[2,128]{1,0:T(2,128)} %param.21) | copy-start | bytes 3076
  (12 other events, 21.0 us)
where the time goes:
time: 491 us; the launch traced here: 482 us
  local copies, waits for them, and re-layouts  134 us (27%)
  matrix products  120 us (24%)
  other arithmetic  110 us (22%)
  waiting for transfers between devices  82.3 us (17%)
  starting transfers between devices  31.6 us (6%)
    dot_general x6, matrix products, one_block(): jnp.einsum('jtkc,jfkc->tfc', powers, coeffs, precision=lax.Precision.HIGH...  120 us
    all_to_all x1, waiting for transfers between devices, local(): lax.all_to_all(occupied[None, :], ('gx', 'gy'), split_axis=1, concat_axis...  54.7 us
    add x2, other arithmetic, fold_edges(): inner + jnp.where(phase == 0, before, 0.0)  45.5 us
    all_to_all x1, waiting for transfers between devices, local(): lax.all_to_all(outgoing, ('gx', 'gy'), split_axis=1, concat_axis=1, tiled...  17.8 us
    slice x3, local copies, waits for them, and re-layouts, with_halo(): last = lax.slice_in_dim(shard, length - width, length, axis=dim)  15.7 us
    while x3, local copies, waits for them, and re-layouts, remap_columns(): lax.map(one_block, target_blocks)  13.9 us
    dynamic_update_slice x12, local copies, waits for them, and re-layouts, remap_columns(): lax.map(one_block, target_blocks)  13.5 us
    reshape x2, local copies, waits for them, and re-layouts, local(): fields_new.reshape(nfields, number_of_layers_total, columns)  10.1 us
  transfers between devices with their start and end apart: 9, of which 3 were waited for; matrix products, arithmetic and copies ran while one was open for 47% of the time, Pallas kernels for 0%

commit v1 on v0

v1 whole, which is shorter than its diff:
```python
import numpy as np
import jax
import jax.numpy as jnp
from jax import lax
from jax.experimental import pallas as pl
from jax.experimental.pallas import tpu as pltpu
from jax.sharding import PartitionSpec as P

NP = 4
top_pressure = 0.002
mid_pressure = 0.6
kappa_sat = 0.06
phase_change_warming = 0.25
auto_rate = 0.8
accrete_rate = 0.5
fall_rate = 20.0
THICK_MIN = 0.005376344
THICK_MAX = 0.017204301

LANES = 128
HALF = LANES // 2
PART = LANES // NP
TYPES = NP - 1
PARAMS = 6
VM = pl.BlockSpec(memory_space=pltpu.VMEM)
ANY = pl.BlockSpec(memory_space=pl.ANY)
F32 = jnp.float32
BF16 = jnp.bfloat16


def params(vmem=48):
    return pltpu.CompilerParams(vmem_limit_bytes=vmem * 1024 * 1024)


def cost(us):
    return pl.CostEstimate(flops=0, bytes_accessed=int(us * 3.0e6), transcendentals=0)


def source_windows(levels):
    slack = 1e-4
    lo, hi = THICK_MIN * (1 - slack), THICK_MAX * (1 + slack)
    k = np.arange(levels)
    surfaces = np.linspace(top_pressure + levels * lo, top_pressure + levels * hi, 4001)[:, None]
    least = np.maximum(top_pressure + lo * k, surfaces - hi * (levels - k))
    most = np.minimum(top_pressure + hi * k, surfaces - lo * (levels - k))
    out = []
    for t in range(1, levels + 1):
        s = t / levels
        p = top_pressure * (1 - s) + s * s * surfaces + s * (1 - s) * mid_pressure
        first = np.min(np.sum(most <= p, axis=1)) - 1
        last = np.max(np.sum(least <= p, axis=1)) - 1
        out.append((max(int(first) - 1, 0), min(int(last) + 1, levels - 1)))
    return out


def tile_windows(levels):
    per_edge = source_windows(levels)
    tiles = -(-levels // 8)
    out = []
    for j in range(tiles):
        rows = per_edge[8 * j : min(8 * j + 8, levels)]
        out.append((min(r[0] for r in rows), max(r[1] for r in rows)))
    return out


def pack_matrix():
    m = np.zeros((NP * LANES, TYPES * LANES), np.float32)
    for b in range(NP):
        for e in range(PART):
            m[b * LANES + NP * e, b * PART + e] = 1
            if e:
                m[b * LANES + NP * e - 1, b * PART + e] = 1
            m[b * LANES + NP * e + 1, LANES + b * PART + e] = 1
            m[b * LANES + NP * e + 2, 2 * LANES + b * PART + e] = 1
    return m


def weight_matrix():
    m = np.zeros((LANES, LANES), np.float32)
    for e in range(PART):
        for base in (0, 3 * PART):
            m[NP * e, base + e] = 1
            if e:
                m[NP * e - 1, base + e] = 1
        m[NP * e + 1, PART + e] = 1
        m[NP * e + 2, 2 * PART + e] = 1
    return m


def split2(x):
    top = x.astype(BF16)
    return top, (x - top.astype(F32)).astype(BF16)


def dot(a, b):
    return jnp.dot(a, b, preferred_element_type=F32)


def select_dot2(x, m):
    rows = x.shape[0]
    top, low = split2(x)
    return dot(top, m) + dot(low, m)


def select_dot3(x, m):
    top = x.astype(BF16)
    rest = x - top.astype(F32)
    mid = rest.astype(BF16)
    low = (rest - mid.astype(F32)).astype(BF16)
    return dot(top, m) + dot(mid, m) + dot(low, m)


def lane_iota(rows):
    return lax.broadcasted_iota(jnp.int32, (rows, LANES), 1)


def row_iota(rows):
    return lax.broadcasted_iota(jnp.int32, (rows, LANES), 0)


def pick_lanes(x, index):
    return jnp.take_along_axis(x, index, axis=1, mode="promise_in_bounds")


def prefix_rows(x):
    tiles = x.shape[0] // 8
    row = row_iota(8)
    carry = jnp.zeros((8, LANES), F32)
    out = []
    for j in range(tiles):
        part = x[8 * j : 8 * j + 8]
        for step in (1, 2, 4):
            part = part + jnp.where(row >= step, pltpu.roll(part, step, 0), 0.0)
        part = part + carry
        carry = jnp.broadcast_to(part[7:8], (8, LANES))
        out.append(part)
    return jnp.concatenate(out, 0)


def field_rows(dyn, trc, levels, which, x):
    source, index = which
    ref = dyn if source == 0 else trc
    return ref[pl.ds(index * 2 * levels + x, levels, stride=2), :]


def pack_quad(dyn, trc, weight, m, quad, x, levels):
    rows = jnp.concatenate(
        [weight[x] * field_rows(dyn, trc, levels, which, x) for which in quad], 1
    )
    return select_dot2(rows, m)


def flat(ref):
    lead = 1
    for size in ref.shape[:-1]:
        lead *= size
    return ref.reshape(lead, LANES)


def first_kernel(levels, quad, ndyn, ntrc, dyn4, trc4, thick3, area_ref, m_ref, mw_ref, up_ref, down_ref, edge_ref):
    dyn, trc, thick = flat(dyn4), flat(trc4), flat(thick3)
    weight = [area_ref[x : x + 1, :] * thick[pl.ds(x, levels, stride=2), :] for x in range(2)]
    m = m_ref[...]
    for x, out in ((0, down_ref), (1, up_ref)):
        packed = pack_quad(dyn, trc, weight, m, quad, x, levels)
        for kind in range(TYPES):
            out[kind, 0:levels, :] = packed[:, kind * LANES : (kind + 1) * LANES]
        out[TYPES, 0:levels, :] = select_dot3(weight[x], mw_ref[...])
        area = jnp.broadcast_to(area_ref[x : x + 1, :], (8, LANES))
        out[TYPES, levels : levels + 1, :] = select_dot3(area, mw_ref[...])[0:1]
    lane = lane_iota(levels)
    ends = jnp.where(lane < HALF, 0, LANES - 1)
    spot = lane % HALF
    fields = [(0, i) for i in range(ndyn)] + [(1, i) for i in range(ntrc)]
    for x in range(2):
        total = jnp.zeros((levels, LANES), F32)
        for number, which in enumerate(fields):
            here = pick_lanes(field_rows(dyn, trc, levels, which, x), ends)
            total = jnp.where(spot == number, here, total)
        both = pick_lanes(weight[x], ends)
        total = jnp.where(spot == len(fields), 1.0, total) * both
        edge_ref[x, 0:levels, :] = total
        edge_ref[x, levels : levels + 1, :] = pick_lanes(
            jnp.broadcast_to(area_ref[x : x + 1, :], (8, LANES)), ends[0:8]
        )[0:1]


def pack_kernel(levels, chunks, dyn4, trc4, thick3, area_ref, m_ref, *outs):
    dyn, trc, thick = flat(dyn4), flat(trc4), flat(thick3)
    weight = [area_ref[x : x + 1, :] * thick[pl.ds(x, levels, stride=2), :] for x in range(2)]
    m = m_ref[...]
    for number, quads in enumerate(chunks):
        up_ref, down_ref = outs[2 * number], outs[2 * number + 1]
        for i, quad in enumerate(quads):
            for x, out in ((0, down_ref), (1, up_ref)):
                packed = pack_quad(dyn, trc, weight, m, quad, x, levels)
                for kind in range(TYPES):
                    out[TYPES * i + kind, 0:levels, :] = packed[:, kind * LANES : (kind + 1) * LANES]


def edge_kernel(own_ref, before_ref, after_ref, row0_ref, row1_ref):
    left = lane_iota(own_ref.shape[1]) < HALF
    for x, out in ((0, row0_ref), (1, row1_ref)):
        out[...] = own_ref[x] + jnp.where(
            left, pltpu.roll(before_ref[x], HALF, 1), pltpu.roll(after_ref[x], HALF, 1)
        )


def remap_group(levels, windows, summed, rm, thick, al, ar, aq, rdt, tile_of, row_of, s_ref):
    rows = summed.shape[0]
    tiles = rows // 8
    q = summed * rm
    first = q[0:1]
    last = jnp.broadcast_to(q[levels - 1 : levels], (rows - levels + 2, LANES))
    s_ref[0, 8 : 8 + rows, :] = q
    s_ref[0, 7:8, :] = first
    s_ref[0, 8 + levels : 10 + rows, :] = last
    below = s_ref[0, 7 : 7 + rows, :]
    q = s_ref[0, 8 : 8 + rows, :]
    above = s_ref[0, 9 : 9 + rows, :]
    above_two = s_ref[0, 10 : 10 + rows, :]
    edge = 7.0 / 12.0 * (q + above) - 1.0 / 12.0 * (below + above_two)
    edge = jnp.clip(edge, jnp.minimum(q, above), jnp.maximum(q, above))
    s_ref[1, 8 : 8 + rows, :] = edge
    s_ref[1, 7:8, :] = first
    left = s_ref[1, 7 : 7 + rows, :]
    layer = thick * q
    through = prefix_rows(layer) - layer
    for j in range(tiles):
        low, high = windows[j][0] // 8, windows[j][1] // 8
        part = slice(8 * j, 8 * j + 8)
        tile, row = tile_of[part], row_of[part]
        got = None
        for v in range(low, high + 1):
            here = [
                jnp.take_along_axis(a[8 * v : 8 * v + 8], row, axis=0, mode="promise_in_bounds")
                for a in (through, left, edge, q)
            ]
            if got is None:
                got = here
            else:
                got = [jnp.where(tile == v, new, old) for new, old in zip(here, got)]
        s_ref[2, 8 + 8 * j : 16 + 8 * j, :] = (
            got[0] + al[part] * got[1] + ar[part] * got[2] + aq[part] * got[3]
        )
    s_ref[2, 7:8, :] = jnp.zeros((1, LANES), F32)
    return (s_ref[2, 8 : 8 + rows, :] - s_ref[2, 7 : 7 + rows, :]) * rdt


def column_surface(weights_surface, edge_surface):
    lane = lane_iota(8)
    spot, kind = lane // NP, lane % NP
    index = jnp.where(kind == 3, jnp.minimum(spot + 1, PART - 1), kind * PART + spot)
    inner = pick_lanes(weights_surface, index)
    return jnp.where((lane == 0) | (lane == LANES - 1), edge_surface, inner)


def setup_kernel(levels, nfields, own0, own1, from_up, from_down, row0, row1, edge_up, edge_down, p_ref, i_ref, e_ref, surface_ref, s_ref):
    windows = tile_windows(levels)
    rows = row0.shape[0]
    tiles = rows // 8
    row = row_iota(rows)
    lane = lane_iota(rows)
    inside = row < levels
    edge_lanes = jnp.where(lane < HALF, nfields, HALF + nfields)
    kept = []
    for base in range(4):
        x = base % 2
        own, got = ((own0, from_up), (own1, from_down))[x]
        eown, egot = ((row0, edge_up), (row1, edge_down))[x]
        if base < 2:
            mass = own[TYPES] + got[TYPES]
        else:
            summed = eown[...] + egot[...]
            mass = pick_lanes(summed, edge_lanes)
        area = mass[levels : levels + 1]
        mass = jnp.where(inside, mass, 1.0)
        thick = jnp.where(inside, mass / area, 1.0)
        after = top_pressure + prefix_rows(thick)
        surface = after[levels - 1 : levels]
        s_ref[0, 8 : 8 + rows, :] = after
        s_ref[0, 7:8, :] = jnp.full((1, LANES), top_pressure, F32)
        s_ref[1, 0:rows, :] = thick
        sigma = (row + 1).astype(F32) / levels
        sigma0 = row.astype(F32) / levels

        def target_at(s):
            return top_pressure * (1.0 - s) + s * s * surface + s * (1.0 - s) * mid_pressure

        target = target_at(sigma)
        rdt = jnp.where(inside, 1.0 / (target - target_at(sigma0)), 1.0)
        index, start, depth = [], [], []
        for j in range(tiles):
            low, high = windows[j]
            here = target[8 * j : 8 * j + 8]
            count = jnp.full((8, LANES), low, jnp.int32)
            source = jnp.broadcast_to(s_ref[0, 7 + low : 8 + low, :], (8, LANES))
            size = jnp.broadcast_to(s_ref[1, low : low + 1, :], (8, LANES))
            for k in range(low + 1, high + 1):
                edge_k = jnp.broadcast_to(s_ref[0, 7 + k : 8 + k, :], (8, LANES))
                size_k = jnp.broadcast_to(s_ref[1, k : k + 1, :], (8, LANES))
                reached = edge_k <= here
                count = jnp.where(reached, k, count)
                source = jnp.where(reached, edge_k, source)
                size = jnp.where(reached, size_k, size)
            index.append(count)
            start.append(source)
            depth.append(size)
        index, start, depth = (jnp.concatenate(a, 0) for a in (index, start, depth))
        f = jnp.clip((target - start) / depth, 0.0, 1.0)
        f2, f3 = f * f, f * f * f
        values = [
            1.0 / mass,
            thick,
            depth * (f - 2.0 * f2 + f3),
            depth * (f3 - f2),
            depth * (3.0 * f2 - 2.0 * f3),
            rdt,
        ]
        tile_of, row_of = index >> 3, index & 7
        if base < 2:
            for kind in range(TYPES):
                lanes = kind * PART + lane % PART
                group = 2 * kind + x
                for i, value in enumerate(values):
                    p_ref[group, i] = pick_lanes(value, lanes)
                i_ref[group, 0] = pick_lanes(tile_of, lanes)
                i_ref[group, 1] = pick_lanes(row_of, lanes)
            kept.append(jnp.broadcast_to(surface, (8, LANES)))
        else:
            e_ref[x] = remap_group(levels, windows, summed, *values, tile_of, row_of, s_ref)
            surface_ref[0:1, x * LANES : (x + 1) * LANES] = column_surface(
                kept[x], jnp.broadcast_to(surface, (8, LANES))
            )[0:1]


def remap_kernel(levels, quads, aliased, own0, own1, from_up, from_down, p_ref, i_ref, e_ref, mt_ref, *rest):
    if aliased:
        rest = rest[2:]
        dyn_ref, trc_ref = rest[:2]
        columns_ref = None
        rest = rest[2:]
    else:
        dyn_ref, trc_ref, columns_ref = rest[:3]
        rest = rest[3:]
    s_ref, packed_ref, out_ref, sems = rest
    windows = tile_windows(levels)
    rows = e_ref.shape[1]
    lane = lane_iota(levels)
    ends = (lane == 0) | (lane == LANES - 1)
    half = jnp.where(lane < HALF, 0, HALF)
    out_rows = flat(out_ref)
    fields = TYPES + 1

    ndyn = sum(1 for which in sum(quads, []) if which[0] == 0)

    def numbers(i, b):
        source, index = quads[0][b]
        first = index + (0 if source == 0 else 3)
        return first

    def one_quad(i, edge_lane):
        for kind in range(TYPES):
            for x in range(2):
                group = 2 * kind + x
                own, got = ((own0, from_up), (own1, from_down))[x]
                summed = own[TYPES * i + kind] + got[TYPES * i + kind]
                values = [p_ref[group, n] for n in range(PARAMS)]
                packed_ref[x * rows : (x + 1) * rows, kind * LANES : (kind + 1) * LANES] = remap_group(
                    levels, windows, summed, *values, i_ref[group, 0], i_ref[group, 1], s_ref.at[x]
                )
        wide = select_dot2(packed_ref[...], mt_ref[...])
        for b in range(fields):
            for x in range(2):
                value = wide[x * rows : x * rows + levels, b * LANES : (b + 1) * LANES]
                outer = pick_lanes(e_ref[x, 0:levels, :], half + edge_lane(b))
                value = jnp.where(ends, outer, value)
                out_rows[pl.ds((i * fields + b) * 2 * levels + x, levels, stride=2), :] = value
                if columns_ref is not None:
                    columns_ref[b, 0:levels, x * LANES : (x + 1) * LANES] = value

    table = [[index + (0 if source == 0 else 3) for source, index in quad] for quad in quads]
    copies = []
    for i, quad in enumerate(quads):
        if i == 0 or len(quads) == 1:
            pass
    if len(quads) == 1:
        one_quad(0, lambda b: table[0][b])
    else:
        steps = [table[i][b] - 4 * i for i in range(len(quads)) for b in range(fields)]
        base = table[0]
        regular = all(table[i][b] == base[b] + 4 * i for i in range(len(quads)) for b in range(fields))
        if regular:

            @pl.loop(0, len(quads))
            def _(i):
                one_quad(i, lambda b: base[b] + 4 * i)
        else:
            one_quad(0, lambda b: table[0][b])
            later = table[1]

            @pl.loop(1, len(quads))
            def _(i):
                one_quad(i, lambda b: later[b] + 4 * (i - 1))

    for i, quad in enumerate(quads):
        b = 0
        while b < fields:
            source, index = quad[b]
            length = 1
            while b + length < fields and quad[b + length] == (source, index + length):
                length += 1
            target = dyn_ref if source == 0 else trc_ref
            copies.append(
                pltpu.make_async_copy(
                    out_ref.at[pl.ds(i * fields + b, length)],
                    target.at[pl.ds(index, length)],
                    sems.at[len(copies)],
                )
            )
            b += length
    for copy in copies:
        copy.start()
    for copy in copies:
        copy.wait()


def turn(row):
    return jnp.transpose(jnp.broadcast_to(row, (LANES, LANES)))


def route_kernel(devices, owner_ref, counts_ref, position_ref):
    capacity = 2 * 2 * LANES // devices
    owner = owner_ref[...].astype(F32)
    rows = [owner[x : x + 1] for x in range(2)]
    down = [turn(r) for r in rows]
    r, c = row_iota(LANES), lane_iota(LANES)
    ranks = []
    for x in range(2):
        same = jnp.where((down[x] == rows[x]) & (r < c), 1.0, 0.0)
        rank = jnp.sum(same, axis=0, keepdims=True)
        if x == 1:
            rank = rank + jnp.sum(jnp.where(down[0] == rows[1], 1.0, 0.0), axis=0, keepdims=True)
        ranks.append(rank)
        position_ref[0:1, x * LANES : (x + 1) * LANES] = (rows[x] * capacity + rank).astype(jnp.int32)
    device = lax.broadcasted_iota(jnp.int32, (devices, LANES), 0).astype(F32)
    count = sum(
        jnp.sum(jnp.where(device == row, 1.0, 0.0), axis=1, keepdims=True) for row in rows
    )
    counts_ref[...] = jnp.broadcast_to(count[:, :, None], (devices, 1, LANES))


def slot_rows(devices, counts_ref, columns):
    capacity = 2 * columns // devices
    slots = devices * capacity
    counts = jnp.concatenate([counts_ref[d] for d in range(devices)], 0)
    r = lax.broadcasted_iota(jnp.int32, (slots, devices), 0) // capacity
    d = lax.broadcasted_iota(jnp.int32, (slots, devices), 1)
    before = dot(jnp.where(d < r, 1.0, 0.0).astype(BF16), counts.astype(BF16))
    own = dot(jnp.where(d == r, 1.0, 0.0).astype(BF16), counts.astype(BF16))
    rank = (lax.broadcasted_iota(jnp.int32, (slots, LANES), 0) % capacity).astype(F32)
    slot = jnp.where(rank < own, before + rank, -1.0).astype(jnp.int32)
    parts = [
        jnp.where(slot == lane_iota(slots) + LANES * g, 1.0, 0.0) for g in range(columns // LANES)
    ]
    return jnp.concatenate(parts, 1).astype(BF16)


def three_parts(x):
    top = x.astype(BF16)
    rest = x - top.astype(F32)
    mid = rest.astype(BF16)
    return top, mid, (rest - mid.astype(F32)).astype(BF16)


def dot_nt(a, b):
    return lax.dot_general(a, b, (((1,), (1,)), ((), ())), preferred_element_type=F32)


def dot_tn(a, b):
    return lax.dot_general(a, b, (((0,), (0,)), ((), ())), preferred_element_type=F32)


def to_slots(hot, values):
    return sum(dot_nt(hot, part) for part in three_parts(values))


def from_slots(hot, values):
    turned = jnp.transpose(values)
    return sum(dot(part, hot) for part in three_parts(turned))


def pad_rows(x):
    return jnp.concatenate([x, jnp.zeros((LANES - x.shape[0], x.shape[1]), x.dtype)], 0)


def cloud_kernel(devices, counts_ref, cloud_ref, send_ref):
    hot = slot_rows(devices, counts_ref, cloud_ref.shape[1])
    send_ref[...] = to_slots(hot, pad_rows(cloud_ref[...]))


def final_kernel(devices, levels, counts_ref, got_ref, cloud_ref):
    hot = slot_rows(devices, counts_ref, cloud_ref.shape[1])
    cloud_ref[...] = from_slots(hot, got_ref[...])[0:levels]


def physics_kernel(levels, columns_ref, got_ref, position_ref, surface_ref, warm_ref, inc_ref, send_ref, a_ref, g_ref):
    columns = position_ref.shape[1]
    slots = got_ref.shape[0]
    hot = jnp.where(
        position_ref[...] == lax.broadcasted_iota(jnp.int32, (slots, columns), 0), 1.0, 0.0
    ).astype(BF16)
    cloud = from_slots(hot, got_ref[...])[0:levels]
    t, v, c, r = (columns_ref[b, 0:levels, :] for b in range(4))
    surface = surface_ref[...]
    row = lax.broadcasted_iota(jnp.int32, (levels, columns), 0)

    def target_at(s):
        return top_pressure * (1.0 - s) + s * s * surface + s * (1.0 - s) * mid_pressure

    upper = target_at(row.astype(F32) / levels)
    lower = target_at((row + 1).astype(F32) / levels)
    layer = lower - upper
    middle = 0.5 * (lower + upper)
    celsius = 10.0 * t
    saturation = 3.8 / middle * jnp.exp(17.27 * celsius / (celsius + 237.3))
    condensed = jnp.maximum((v - saturation) / (1.0 + kappa_sat * saturation), -c)
    v1 = v - condensed
    c1 = c + condensed
    t1 = t + phase_change_warming * condensed
    converted = c1 * (1.0 - jnp.exp(-(auto_rate * cloud + accrete_rate * r)))
    warm_rows = warm_ref[...]
    warm = jnp.concatenate([warm_rows[0:1], warm_rows[1:2]], 1) == 1
    c2 = jnp.where(warm, c1 - converted, c1)
    r1 = jnp.where(warm, r + converted, r)
    fall = fall_rate * (0.5 + cloud)
    share = 1.0 / (1.0 + fall)
    a_ref[0:levels, :] = r1 * layer
    g_ref[0:levels, :] = fall * share
    held = jnp.zeros((1, columns), F32)
    for k in range(levels):
        held = a_ref[k : k + 1, :] + held
        a_ref[k : k + 1, :] = held
        held = g_ref[k : k + 1, :] * held
    r2 = jnp.where(warm, a_ref[0:levels, :] * share / layer, r1)
    out = flat(inc_ref)
    for b, change in enumerate((t1 - t, v1 - v, c2 - c, r2 - r)):
        for x in range(2):
            out[pl.ds(b * 2 * levels + x, levels, stride=2), :] = change[:, x * LANES : (x + 1) * LANES]
    goal = jnp.clip((v1 / saturation - 0.7) / 0.3, 0.05, 1.0)
    send_ref[...] = to_slots(hot, pad_rows(cloud + 0.5 * (goal - cloud)))


def ring(axis):
    size = lax.axis_size(axis)
    up = [(i, (i + 1) % size) for i in range(size)]
    return up, [(j, i) for i, j in up]


def shape(*dims, dtype=F32):
    return jax.ShapeDtypeStruct(dims, dtype)


def local(dynamics, tracers, thickness, area_weight, cloud_frac, owner, warm_mask):
    levels = thickness.shape[0]
    ndyn, ntrc = dynamics.shape[0], tracers.shape[0]
    nfields = ndyn + ntrc
    rows = -(-(levels + 1) // 8) * 8
    columns = 2 * LANES
    devices = lax.axis_size(("gx", "gy"))
    slots = devices * (2 * columns // devices)
    axes = ("gx", "gy")
    fields = [(0, i) for i in range(1, ndyn)] + [(1, i) for i in range(3, ntrc)]
    quads = [fields[i : i + 4] for i in range(0, len(fields), 4)]
    first_quad = [(0, 0), (1, 0), (1, 1), (1, 2)]
    chunks = [quads[:4], quads[4:]]
    matrix = pack_matrix()
    m = jnp.asarray(matrix, BF16)
    mt = jnp.asarray(matrix.T, BF16)
    mw = jnp.asarray(weight_matrix(), BF16)
    up, down = ring("gx")
    right, left = ring("gy")

    counts, position = pl.pallas_call(
        lambda *refs: route_kernel(devices, *refs),
        out_shape=(shape(devices, 1, LANES), shape(1, columns, dtype=jnp.int32)),
        in_specs=[VM],
        out_specs=(VM, VM),
        compiler_params=params(),
        cost_estimate=cost(1),
        name="route",
    )(owner)
    counts_in = lax.all_to_all(counts, axes, split_axis=0, concat_axis=0, tiled=True)

    up0, down0, edges = pl.pallas_call(
        lambda *refs: first_kernel(levels, first_quad, ndyn, ntrc, *refs),
        out_shape=(shape(TYPES + 1, rows, LANES),) * 2 + (shape(2, rows, LANES),),
        in_specs=[VM] * 6,
        out_specs=(VM,) * 3,
        compiler_params=params(),
        cost_estimate=cost(4),
        name="first_pack",
    )(dynamics, tracers, thickness, area_weight, m, mw)
    before = lax.ppermute(edges, "gy", right)
    after = lax.ppermute(edges, "gy", left)
    from_up0 = lax.ppermute(up0, "gx", up)
    from_down0 = lax.ppermute(down0, "gx", down)

    packed = pl.pallas_call(
        lambda *refs: pack_kernel(levels, chunks, *refs),
        out_shape=tuple(shape(TYPES * len(c), rows, LANES) for c in chunks for _ in range(2)),
        in_specs=[VM] * 5,
        out_specs=(VM,) * (2 * len(chunks)),
        compiler_params=params(),
        cost_estimate=cost(6),
        name="pack",
    )(dynamics, tracers, thickness, area_weight, m)

    row0, row1 = pl.pallas_call(
        edge_kernel,
        out_shape=(shape(rows, LANES),) * 2,
        in_specs=[VM] * 3,
        out_specs=(VM,) * 2,
        compiler_params=params(),
        cost_estimate=cost(1),
        name="edge_sum",
    )(edges, before, after)
    edge_up = lax.ppermute(row1, "gx", up)
    edge_down = lax.ppermute(row0, "gx", down)

    cloud_out = pl.pallas_call(
        lambda *refs: cloud_kernel(devices, *refs),
        out_shape=shape(slots, LANES),
        in_specs=[VM] * 2,
        out_specs=VM,
        compiler_params=params(),
        cost_estimate=cost(2),
        name="cloud_send",
    )(counts_in, cloud_frac)
    cloud_in = lax.all_to_all(cloud_out, axes, split_axis=0, concat_axis=0, tiled=True)

    received = []
    for number in range(len(chunks)):
        received.append(
            (
                lax.ppermute(packed[2 * number], "gx", up),
                lax.ppermute(packed[2 * number + 1], "gx", down),
            )
        )

    weights, indices, edge_values, surface = pl.pallas_call(
        lambda *refs: setup_kernel(levels, nfields, *refs),
        out_shape=(
            shape(2 * TYPES, PARAMS, rows, LANES),
            shape(2 * TYPES, 2, rows, LANES, dtype=jnp.int32),
            shape(2, rows, LANES),
            shape(1, columns),
        ),
        in_specs=[VM] * 8,
        out_specs=(VM,) * 4,
        scratch_shapes=[pltpu.VMEM((3, rows + 16, LANES), F32)],
        compiler_params=params(),
        cost_estimate=cost(5),
        name="column_setup",
    )(down0, up0, from_up0, from_down0, row0, row1, edge_up, edge_down)

    def remap(chunk, own0, own1, got_up, got_down, so_far):
        aliased = so_far is not None
        out_shape = (shape(*dynamics.shape), shape(*tracers.shape))
        args = [own0, own1, got_up, got_down, weights, indices, edge_values, mt]
        in_specs = [VM] * 8
        out_specs = (ANY, ANY)
        aliases = {}
        if aliased:
            args += list(so_far)
            in_specs += [ANY, ANY]
            aliases = {8: 0, 9: 1}
        else:
            out_shape += (shape(4, rows, columns),)
            out_specs += (VM,)
        return pl.pallas_call(
            lambda *refs: remap_kernel(levels, chunk, aliased, *refs),
            out_shape=out_shape,
            in_specs=in_specs,
            out_specs=out_specs,
            input_output_aliases=aliases,
            scratch_shapes=[
                pltpu.VMEM((2, 3, rows + 16, LANES), F32),
                pltpu.VMEM((2 * rows, TYPES * LANES), F32),
                pltpu.VMEM((4 * len(chunk), levels, 2, LANES), F32),
                pltpu.SemaphoreType.DMA((2 * len(chunk),)),
            ],
            compiler_params=params(),
            cost_estimate=cost(4 * len(chunk)),
            name="remap",
        )(*args)

    dyn_new, trc_new, physics_columns = remap([first_quad], down0, up0, from_up0, from_down0, None)

    increments, next_out = pl.pallas_call(
        lambda *refs: physics_kernel(levels, *refs),
        out_shape=(shape(4, levels, 2, LANES), shape(slots, LANES)),
        in_specs=[VM] * 5,
        out_specs=(VM,) * 2,
        scratch_shapes=[pltpu.VMEM((rows, columns), F32)] * 2,
        compiler_params=params(),
        cost_estimate=cost(5),
        name="physics",
    )(physics_columns, cloud_in, position, surface, warm_mask)
    next_in = lax.all_to_all(next_out, axes, split_axis=0, concat_axis=0, tiled=True)

    done = (dyn_new, trc_new)
    for number, chunk in enumerate(chunks):
        done = remap(chunk, packed[2 * number + 1], packed[2 * number], *received[number], done)

    cloud_next = pl.pallas_call(
        lambda *refs: final_kernel(devices, levels, *refs),
        out_shape=shape(levels, columns),
        in_specs=[VM] * 2,
        out_specs=VM,
        compiler_params=params(),
        cost_estimate=cost(2),
        name="cloud_receive",
    )(counts_in, next_in)
    return (done[0], done[1], increments, cloud_next)


def solution(mesh):
    placed = (
        P(None, None, "gx", "gy"),
        P(None, None, "gx", "gy"),
        P(None, "gx", "gy"),
        P("gx", "gy"),
        P(None, ("gx", "gy")),
        P("gx", "gy"),
        P("gx", "gy"),
    )
    return jax.shard_map(
        local,
        mesh=mesh,
        in_specs=placed,
        out_specs=(
            P(None, None, "gx", "gy"),
            P(None, None, "gx", "gy"),
            P(None, None, "gx", "gy"),
            P(None, ("gx", "gy")),
        ),
        check_vma=False,
    )
```

time: 491 us -> 108 us (0.22); the launches traced: 482 us -> 108 us
  local copies, waits for them, and re-layouts: 134 us -> 8.48 us
  matrix products: 120 us -> 0 us
  other arithmetic: 110 us -> 0 us
  waiting for transfers between devices: 82.3 us -> 30.2 us
  Pallas kernels: 0 us -> 30.4 us
  blocking collectives: 0 us -> 14.3 us
  starting transfers between devices: 31.6 us -> 23.4 us
    dot_general x6 -> x0, matrix products: 120 us -> none  [one_block(): jnp.einsum('jtkc,jfkc->tfc', powers, coeffs, precision=lax.Precision.HIGH...]
    all_to_all x5 -> x2, waiting for transfers between devices: 82.2 us -> 0.01 us  [the longest x1 0.01 us: local(): lax.all_to_all(cloud_out, axes, split_axis=0, concat_axis=0, tiled=True)]
    add x6 -> x0, other arithmetic: 53.4 us -> none  [the longest x2 45.5 us: fold_edges(): inner + jnp.where(phase == 0, before, 0.0)]
    pallas_call x0 -> x11, Pallas kernels: none -> 30.4 us  [the longest x3 17.9 us: remap(): pl.pallas_call(lambda *refs: remap_kernel(levels, chunk, aliased, *refs),...]
    ppermute x4 -> x10, waiting for transfers between devices: 0.01 us -> 30.2 us  [the longest x2 21.9 us: local(): lax.ppermute(packed[2 * number + 1], 'gx', down)]
    slice x10 -> x0, local copies, waits for them, and re-layouts: 24.2 us -> none  [the longest x3 15.7 us: with_halo(): last = lax.slice_in_dim(shard, length - width, length, axis=dim)]
    gather x8 -> x0, local copies, waits for them, and re-layouts: 18.5 us -> none  [the longest x1 4.79 us: local(): out_warm = (warm_cols[sources] * occupied)[None, :]]
    all_to_all x5 -> x2, starting transfers between devices: 23.3 us -> 5.35 us  [the longest x1 2.76 us: local(): lax.all_to_all(next_out, axes, split_axis=0, concat_axis=0, tiled=True)]
  transfers between devices with their start and end apart: 9 -> 12, of which waited for: 3 -> 5; matrix products, arithmetic and copies ran while one was open for 47% -> 0% of each run, Pallas kernels for 0% -> 26%
where the time goes in v1:
time: 108 us
  Pallas kernels  30.4 us (28%)
  waiting for transfers between devices  30.2 us (28%)
  starting transfers between devices  23.4 us (22%)
  blocking collectives  14.3 us (13%)
  local copies, waits for them, and re-layouts  8.48 us (8%)
    ppermute x2, waiting for transfers between devices, local(): lax.ppermute(packed[2 * number + 1], 'gx', down)  21.9 us
    pallas_call x3, Pallas kernels, remap(): pl.pallas_call(lambda *refs: remap_kernel(levels, chunk, aliased, *refs),...  17.9 us
    all_to_all x1, blocking collectives, local(): lax.all_to_all(counts, axes, split_axis=0, concat_axis=0, tiled=True)  14.3 us
    unnamed x26, local copies, waits for them, and re-layouts  8.48 us
    ppermute x2, waiting for transfers between devices, local(): lax.ppermute(packed[2 * number], 'gx', up)  8.15 us
    ppermute x2, starting transfers between devices, local(): lax.ppermute(packed[2 * number + 1], 'gx', down)  7.65 us
    pallas_call x1, Pallas kernels, local(): pl.pallas_call(lambda *refs: pack_kernel(levels, chunks, *refs), out_shap...  5.12 us
    all_to_all x1, starting transfers between devices, local(): lax.all_to_all(next_out, axes, split_axis=0, concat_axis=0, tiled=True)  2.76 us
  transfers between devices with their start and end apart: 12, of which 5 were waited for; matrix products, arithmetic and copies ran while one was open for 0% of the time, Pallas kernels for 26%

profile of v1, /device:TPU:0, one launch (start us, length us, event | category | flops | bytes accessed | tf_op | source)
XLA Modules:
  0.0 107.6 jit_solution(10571789649633434767)
XLA Ops:
  0.7 0.7 copy-done.12
  1.5 14.3 %all_to_all.27.refs_0_ = f32[32,1,128]{2,1,0:T(1,128)S(1)} all-to-all(f32[32,1,128]{2,1,0:T(1,128)S(1)} %get-tuple-element.47), channel_id=1, replica_groups=mesh['gx'=4,'gy'=8] {'gx','gy'}, dimensions={0} | all-to-all | bytes 32768 | tf_op jit(solution)/shard_map/all_to_all | solution.py:593
  15.8 0.9 copy-done.7
  16.7 1.2 %cloud_send.1 = f32[512,128]{1,0:T(8,128)} custom-call(f32[32,1,128]{2,1,0:T(1,128)S(1)} %all_to_all.27.refs_0_, f32[93,256]{1,0:T(8,128)S(1)} %copy-done.7), custom_call_target="tpu_custom_call" | custom-call | bytes 6000000 | tf_op jit(solution)/shard_map/cloud_send/pallas_call | solution.py:631
  17.9 2.6 %all-to-all-start.1 = ((f32[32,16,128]{2,1,0:T(8,128)}), f32[32,16,128]{2,1,0:T(8,128)S(1)}, u32[]{:S(2)}, u32[]{:S(2)}) async-start(f32[32,16,128]{2,1,0:T(8,128)} %bitcast), calls=%async_computation.1 | async-start | bytes 524288 | tf_op jit(solution)/shard_map/all_to_all | solution.py:640
  20.5 1.9 %copy-done = f32[33,93,2,128]{3,2,1,0:T(2,128)S(1)} copy-done((f32[33,93,2,128]{3,2,1,0:T(2,128)S(1)}, f32[33,93,2,128]{3,2,1,0:T(2,128)}, u32[]{:S(2)}) %copy-start) | copy-done | bytes 3142680
  22.4 1.0 copy-done.2
  23.4 1.0 copy-done.3
  24.4 0.9 copy-done.5
  25.2 0.8 copy-done.8
  26.0 0.7 copy-done.9
  26.7 1.1 %first_pack.1 = (f32[4,96,128]{2,1,0:T(8,128)S(1)}, f32[4,96,128]{2,1,0:T(8,128)S(1)}, f32[2,96,128]{2,1,0:T(8,128)S(1)}) custom-call(f32[3,93,2,128]{3,2,1,0:T(2,128)S(1)} %copy-done.3, f32[33,93,2,128]{3,2,1,0:T(2,128)S(1)} %copy-done, f32[93,2,128]{2,1,0:T(2,128)S(1)} %copy-done.5, f32[2,128]{1,0:T(2,128)S(1)} %copy-done.9, ...), custom_call_target="tpu_custom_call" | custom-call | bytes 12000000 | tf_op jit(solution)/shard_map/first_pack/pallas_call | solution.py:595
  27.8 1.7 %collective-permute-start.2 = (f32[4,96,128]{2,1,0:T(8,128)S(1)}, f32[4,96,128]{2,1,0:T(8,128)S(1)}, u32[]{:S(2)}, u32[]{:S(2)}) collective-permute-start(f32[4,96,128]{2,1,0:T(8,128)S(1)} %get-tuple-element.31.refs_1_), channel_id=1, source_target_pairs={{0,8},{8,16},{16,24},{24,0},{1,9},{9,17},{17,25},{25,1},{2,10},{10... | collective-permute-start | bytes 589832 | tf_op jit(solution)/shard_map/ppermute | solution.py:606
  29.6 2.6 %collective-permute-start.5 = (f32[2,96,128]{2,1,0:T(8,128)S(1)}, f32[2,96,128]{2,1,0:T(8,128)S(1)}, u32[]{:S(2)}, u32[]{:S(2)}) collective-permute-start(f32[2,96,128]{2,1,0:T(8,128)S(1)} %get-tuple-element.32.own_ref), channel_id=1, source_target_pairs={{1,0},{2,1},{3,2},{4,3},{5,4},{6,5},{7,6},{0,7},{9,8},{10,9},{11,1... | collective-permute-start | bytes 294920 | tf_op jit(solution)/shard_map/ppermute | solution.py:605
  32.2 2.1 %collective-permute-start.3 = (f32[4,96,128]{2,1,0:T(8,128)S(1)}, f32[4,96,128]{2,1,0:T(8,128)S(1)}, u32[]{:S(2)}, u32[]{:S(2)}) collective-permute-start(f32[4,96,128]{2,1,0:T(8,128)S(1)} %get-tuple-element.30.refs_0_), channel_id=1, source_target_pairs={{8,0},{16,8},{24,16},{0,24},{9,1},{17,9},{25,17},{1,25},{10,2},{18... | collective-permute-start | bytes 589832 | tf_op jit(solution)/shard_map/ppermute | solution.py:607
  34.6 1.6 %collective-permute-start.6 = (f32[96,128]{1,0:T(8,128)S(1)}, f32[96,128]{1,0:T(8,128)S(1)}, u32[]{:S(2)}, u32[]{:S(2)}) collective-permute-start(f32[96,128]{1,0:T(8,128)S(1)} %get-tuple-element.34.refs_5_), channel_id=1, source_target_pairs={{0,8},{8,16},{16,24},{24,0},{1,9},{9,17},{17,25},{25,1},{2,10},{10... | collective-permute-start | bytes 147464 | tf_op jit(solution)/shard_map/ppermute | solution.py:628
  36.2 2.3 %collective-permute-start.7 = (f32[96,128]{1,0:T(8,128)S(1)}, f32[96,128]{1,0:T(8,128)S(1)}, u32[]{:S(2)}, u32[]{:S(2)}) collective-permute-start(f32[96,128]{1,0:T(8,128)S(1)} %get-tuple-element.33.refs_4_), channel_id=1, source_target_pairs={{8,0},{16,8},{24,16},{0,24},{9,1},{17,9},{25,17},{1,25},{10,2},{18... | collective-permute-start | bytes 147464 | tf_op jit(solution)/shard_map/ppermute | solution.py:629
  38.5 5.1 %pack.1 = (f32[12,96,128]{2,1,0:T(8,128)}, f32[12,96,128]{2,1,0:T(8,128)}, f32[12,96,128]{2,1,0:T(8,128)}, f32[12,96,128]{2,1,0:T(8,128)}) custom-call(f32[3,93,2,128]{3,2,1,0:T(2,128)S(1)} %copy-done.4, f32[33,93,2,128]{3,2,1,0:T(2,128)} %refs_1_.4, f32[93,2,128]{2,1,0:T(2,128)S(1)} %copy-done.5, f32[2,128]{1,0:T(2,128)S(1)} %copy-done.10, ...), custom_call_target="tpu_custom_call" | custom-call | bytes 18000000 | tf_op jit(solution)/shard_map/pack/pallas_call | solution.py:609
  43.7 3.8 %collective-permute-start.9 = (f32[12,96,128]{2,1,0:T(8,128)}, f32[12,96,128]{2,1,0:T(8,128)}, u32[]{:S(2)}, u32[]{:S(2)}) collective-permute-start(f32[12,96,128]{2,1,0:T(8,128)} %get-tuple-element.38.refs_0_), channel_id=1, source_target_pairs={{8,0},{16,8},{24,16},{0,24},{9,1},{17,9},{25,17},{1,25},{10,2},{18... | collective-permute-start | bytes 1769480 | tf_op jit(solution)/shard_map/ppermute | solution.py:647
  47.5 3.8 %collective-permute-start.1 = (f32[12,96,128]{2,1,0:T(8,128)}, f32[12,96,128]{2,1,0:T(8,128)}, u32[]{:S(2)}, u32[]{:S(2)}) collective-permute-start(f32[12,96,128]{2,1,0:T(8,128)} %get-tuple-element.28.refs_0_), channel_id=1, source_target_pairs={{8,0},{16,8},{24,16},{0,24},{9,1},{17,9},{25,17},{1,25},{10,2},{18... | collective-permute-start | bytes 1769480 | tf_op jit(solution)/shard_map/ppermute | solution.py:647
  51.3 2.1 %column_setup.1 = (f32[6,6,96,128]{3,2,1,0:T(8,128)S(1)}, s32[6,2,96,128]{3,2,1,0:T(8,128)S(1)}, f32[2,96,128]{2,1,0:T(8,128)S(1)}, f32[1,256]{1,0:T(1,128)S(1)}) custom-call(f32[4,96,128]{2,1,0:T(8,128)S(1)} %get-tuple-element.30.refs_0_, f32[4,96,128]{2,1,0:T(8,128)S(1)} %get-tuple-element.31.refs_1_, f32[4,96,128]{2,1,0:T(8,128)S(1)} %collective-permute-done.2.refs_2_, ...), custom_call_target="tpu_custom_call" | custom-call | bytes 15000000 | tf_op jit(solution)/shard_map/column_setup/pallas_call | solution.py:651
  53.5 2.1 %remap.3 = (f32[3,93,2,128]{3,2,1,0:T(2,128)}, f32[33,93,2,128]{3,2,1,0:T(2,128)}, f32[4,96,256]{2,1,0:T(8,128)S(1)}) custom-call(f32[4,96,128]{2,1,0:T(8,128)S(1)} %get-tuple-element.30.refs_0_, f32[4,96,128]{2,1,0:T(8,128)S(1)} %get-tuple-element.31.refs_1_, f32[4,96,128]{2,1,0:T(8,128)S(1)} %collective-permute-done.2.refs_2_, ...), custom_call_target="tpu_custom_call" | custom-call | bytes 12000000 | tf_op jit(solution)/shard_map/remap/pallas_call | solution.py:681
  55.6 1.4 %physics.1 = (f32[4,93,2,128]{3,2,1,0:T(2,128)}, f32[512,128]{1,0:T(8,128)S(1)}) custom-call(f32[4,96,256]{2,1,0:T(8,128)S(1)} %get-tuple-element.46.refs_0_, f32[512,128]{1,0:T(8,128)S(1)} %bitcast.4, s32[1,256]{1,0:T(1,128)S(1)} %get-tuple-element.48.refs_2_, f32[1,256]{1,0:T(1,128)S(1)} %get-tuple-element.49.refs_3_, s32[2,128]{1,0:T(2,128)S(1)} %copy-done.11), custom_call_target="tpu_custom_call" | custom-call | bytes 15000000 | tf_op jit(solution)/shard_map/physics/pallas_call | solution.py:700
  56.9 0.7 copy-done.6
  57.6 2.8 %all-to-all-start.2 = ((f32[32,16,128]{2,1,0:T(8,128)}), f32[32,16,128]{2,1,0:T(8,128)S(1)}, u32[]{:S(2)}, u32[]{:S(2)}) async-start(f32[32,16,128]{2,1,0:T(8,128)} %bitcast.6), calls=%async_computation.2 | async-start | bytes 524288 | tf_op jit(solution)/shard_map/all_to_all | solution.py:710
  60.4 1.6 %collective-permute-done.8.refs_2_ = f32[12,96,128]{2,1,0:T(8,128)} collective-permute-done((f32[12,96,128]{2,1,0:T(8,128)}, f32[12,96,128]{2,1,0:T(8,128)}, u32[]{:S(2)}, u32[]{:S(2)}) %collective-permute-start.8) | collective-permute-done | bytes 589856 | tf_op jit(solution)/shard_map/ppermute | solution.py:646
  62.0 10.9 %collective-permute-done.9.refs_3_ = f32[12,96,128]{2,1,0:T(8,128)} collective-permute-done((f32[12,96,128]{2,1,0:T(8,128)}, f32[12,96,128]{2,1,0:T(8,128)}, u32[]{:S(2)}, u32[]{:S(2)}) %collective-permute-start.9) | collective-permute-done | bytes 589856 | tf_op jit(solution)/shard_map/ppermute | solution.py:647
  72.9 7.9 %remap.4 = (f32[3,93,2,128]{3,2,1,0:T(2,128)}, f32[33,93,2,128]{3,2,1,0:T(2,128)}) custom-call(f32[12,96,128]{2,1,0:T(8,128)} %get-tuple-element.38.refs_0_, f32[12,96,128]{2,1,0:T(8,128)} %get-tuple-element.39.refs_1_, f32[12,96,128]{2,1,0:T(8,128)} %collective-permute-done.8.refs_2_, ...), custom_call_target="tpu_custom_call", output_to_operand_aliasing={{0}: (8, {}), {1}: (9, {})} | custom-call | bytes 48000000 | tf_op jit(solution)/shard_map/remap/pallas_call | solution.py:681
  80.8 6.5 %collective-permute-done.refs_2_ = f32[12,96,128]{2,1,0:T(8,128)} collective-permute-done((f32[12,96,128]{2,1,0:T(8,128)}, f32[12,96,128]{2,1,0:T(8,128)}, u32[]{:S(2)}, u32[]{:S(2)}) %collective-permute-start) | collective-permute-done | bytes 589856 | tf_op jit(solution)/shard_map/ppermute | solution.py:646
  87.3 11.1 %collective-permute-done.1.refs_3_ = f32[12,96,128]{2,1,0:T(8,128)} collective-permute-done((f32[12,96,128]{2,1,0:T(8,128)}, f32[12,96,128]{2,1,0:T(8,128)}, u32[]{:S(2)}, u32[]{:S(2)}) %collective-permute-start.1) | collective-permute-done | bytes 589856 | tf_op jit(solution)/shard_map/ppermute | solution.py:647
  98.4 7.9 %remap.5 = (f32[3,93,2,128]{3,2,1,0:T(2,128)}, f32[33,93,2,128]{3,2,1,0:T(2,128)}) custom-call(f32[12,96,128]{2,1,0:T(8,128)} %get-tuple-element.28.refs_0_, f32[12,96,128]{2,1,0:T(8,128)} %get-tuple-element.29.refs_1_, f32[12,96,128]{2,1,0:T(8,128)} %collective-permute-done.refs_2_, ...), custom_call_target="tpu_custom_call", output_to_operand_aliasing={{0}: (8, {}), {1}: (9, {})} | custom-call | bytes 48000000 | tf_op jit(solution)/shard_map/remap/pallas_call | solution.py:681
  106.4 1.2 %cloud_receive.1 = f32[93,256]{1,0:T(8,128)} custom-call(f32[32,1,128]{2,1,0:T(1,128)S(1)} %all_to_all.27.refs_0_, f32[512,128]{1,0:T(8,128)S(1)} %bitcast.5), custom_call_target="tpu_custom_call" | custom-call | bytes 6000000 | tf_op jit(solution)/shard_map/cloud_receive/pallas_call | solution.py:716
  (30 shorter events, 0.5 us)
Async XLA Ops:
  0.6 37.9 %copy-start.4 = (f32[3,93,2,128]{3,2,1,0:T(2,128)S(1)}, f32[3,93,2,128]{3,2,1,0:T(2,128)}, u32[]{:S(2)}) copy-start(f32[3,93,2,128]{3,2,1,0:T(2,128)} %refs_0_.4) | copy-start | bytes 857092
  0.6 0.7 copy-start.12
  15.8 0.9 copy-start.7
  16.7 21.9 %copy-start.10 = (f32[2,128]{1,0:T(2,128)S(1)}, f32[2,128]{1,0:T(2,128)}, u32[]{:S(2)}) copy-start(f32[2,128]{1,0:T(2,128)} %refs_3_.3) | copy-start | bytes 3076
  17.9 37.6 %all-to-all-start.1 = ((f32[32,16,128]{2,1,0:T(8,128)}), f32[32,16,128]{2,1,0:T(8,128)S(1)}, u32[]{:S(2)}, u32[]{:S(2)}) async-start(f32[32,16,128]{2,1,0:T(8,128)} %bitcast), calls=%async_computation.1 | async-start | bytes 524288 | tf_op jit(solution)/shard_map/all_to_all | solution.py:640
  20.5 1.9 %copy-start = (f32[33,93,2,128]{3,2,1,0:T(2,128)S(1)}, f32[33,93,2,128]{3,2,1,0:T(2,128)}, u32[]{:S(2)}) copy-start(f32[33,93,2,128]{3,2,1,0:T(2,128)} %refs_1_.4) | copy-start | bytes 9427972
  22.4 1.0 copy-start.2
  23.4 1.0 copy-start.3
  24.4 0.9 copy-start.5
  25.2 0.8 copy-start.8
  26.0 0.7 copy-start.9
  27.8 25.6 %copy-start.1 = (bf16[384,512]{1,0:T(8,128)(2,1)S(1)}, bf16[384,512]{1,0:T(8,128)(2,1)}, u32[]{:S(2)}) copy-start(bf16[384,512]{1,0:T(8,128)(2,1)} %constant.7.clone.refs_7_) | copy-start | bytes 1179652
  27.8 19.7 %collective-permute-start.2 = (f32[4,96,128]{2,1,0:T(8,128)S(1)}, f32[4,96,128]{2,1,0:T(8,128)S(1)}, u32[]{:S(2)}, u32[]{:S(2)}) collective-permute-start(f32[4,96,128]{2,1,0:T(8,128)S(1)} %get-tuple-element.31.refs_1_), channel_id=1, source_target_pairs={{0,8},{8,16},{16,24},{24,0},{1,9},{9,17},{17,25},{25,1},{2,10},{10... | collective-permute-start | bytes 589832 | tf_op jit(solution)/shard_map/ppermute | solution.py:606
  29.6 4.9 %collective-permute-start.4 = (f32[2,96,128]{2,1,0:T(8,128)S(1)}, f32[2,96,128]{2,1,0:T(8,128)S(1)}, u32[]{:S(2)}, u32[]{:S(2)}) collective-permute-start(f32[2,96,128]{2,1,0:T(8,128)S(1)} %get-tuple-element.32.own_ref), channel_id=1, source_target_pairs={{0,1},{1,2},{2,3},{3,4},{4,5},{5,6},{6,7},{7,0},{8,9},{9,10},{10,1... | collective-permute-start | bytes 294920 | tf_op jit(solution)/shard_map/ppermute | solution.py:604
  29.6 4.9 %collective-permute-start.5 = (f32[2,96,128]{2,1,0:T(8,128)S(1)}, f32[2,96,128]{2,1,0:T(8,128)S(1)}, u32[]{:S(2)}, u32[]{:S(2)}) collective-permute-start(f32[2,96,128]{2,1,0:T(8,128)S(1)} %get-tuple-element.32.own_ref), channel_id=1, source_target_pairs={{1,0},{2,1},{3,2},{4,3},{5,4},{6,5},{7,6},{0,7},{9,8},{10,9},{11,1... | collective-permute-start | bytes 294920 | tf_op jit(solution)/shard_map/ppermute | solution.py:605
  32.2 19.1 %collective-permute-start.3 = (f32[4,96,128]{2,1,0:T(8,128)S(1)}, f32[4,96,128]{2,1,0:T(8,128)S(1)}, u32[]{:S(2)}, u32[]{:S(2)}) collective-permute-start(f32[4,96,128]{2,1,0:T(8,128)S(1)} %get-tuple-element.30.refs_0_), channel_id=1, source_target_pairs={{8,0},{16,8},{24,16},{0,24},{9,1},{17,9},{25,17},{1,25},{10,2},{18... | collective-permute-start | bytes 589832 | tf_op jit(solution)/shard_map/ppermute | solution.py:607
  34.6 9.0 %collective-permute-start.6 = (f32[96,128]{1,0:T(8,128)S(1)}, f32[96,128]{1,0:T(8,128)S(1)}, u32[]{:S(2)}, u32[]{:S(2)}) collective-permute-start(f32[96,128]{1,0:T(8,128)S(1)} %get-tuple-element.34.refs_5_), channel_id=1, source_target_pairs={{0,8},{8,16},{16,24},{24,0},{1,9},{9,17},{17,25},{25,1},{2,10},{10... | collective-permute-start | bytes 147464 | tf_op jit(solution)/shard_map/ppermute | solution.py:628
  36.2 11.3 %collective-permute-start.7 = (f32[96,128]{1,0:T(8,128)S(1)}, f32[96,128]{1,0:T(8,128)S(1)}, u32[]{:S(2)}, u32[]{:S(2)}) collective-permute-start(f32[96,128]{1,0:T(8,128)S(1)} %get-tuple-element.33.refs_4_), channel_id=1, source_target_pairs={{8,0},{16,8},{24,16},{0,24},{9,1},{17,9},{25,17},{1,25},{10,2},{18... | collective-permute-start | bytes 147464 | tf_op jit(solution)/shard_map/ppermute | solution.py:629
  43.7 11.9 %copy-start.11 = (s32[2,128]{1,0:T(2,128)S(1)}, s32[2,128]{1,0:T(2,128)}, u32[]{:S(2)}) copy-start(s32[2,128]{1,0:T(2,128)} %refs_4_.3) | copy-start | bytes 3076
  43.7 18.4 %collective-permute-start.8 = (f32[12,96,128]{2,1,0:T(8,128)}, f32[12,96,128]{2,1,0:T(8,128)}, u32[]{:S(2)}, u32[]{:S(2)}) collective-permute-start(f32[12,96,128]{2,1,0:T(8,128)} %get-tuple-element.39.refs_1_), channel_id=1, source_target_pairs={{0,8},{8,16},{16,24},{24,0},{1,9},{9,17},{17,25},{25,1},{2,10},{10... | collective-permute-start | bytes 1769480 | tf_op jit(solution)/shard_map/ppermute | solution.py:646
  43.7 29.2 %collective-permute-start.9 = (f32[12,96,128]{2,1,0:T(8,128)}, f32[12,96,128]{2,1,0:T(8,128)}, u32[]{:S(2)}, u32[]{:S(2)}) collective-permute-start(f32[12,96,128]{2,1,0:T(8,128)} %get-tuple-element.38.refs_0_), channel_id=1, source_target_pairs={{8,0},{16,8},{24,16},{0,24},{9,1},{17,9},{25,17},{1,25},{10,2},{18... | collective-permute-start | bytes 1769480 | tf_op jit(solution)/shard_map/ppermute | solution.py:647
  47.5 39.8 %collective-permute-start = (f32[12,96,128]{2,1,0:T(8,128)}, f32[12,96,128]{2,1,0:T(8,128)}, u32[]{:S(2)}, u32[]{:S(2)}) collective-permute-start(f32[12,96,128]{2,1,0:T(8,128)} %get-tuple-element.29.refs_1_), channel_id=1, source_target_pairs={{0,8},{8,16},{16,24},{24,0},{1,9},{9,17},{17,25},{25,1},{2,10},{10... | collective-permute-start | bytes 1769480 | tf_op jit(solution)/shard_map/ppermute | solution.py:646
  47.5 50.9 %collective-permute-start.1 = (f32[12,96,128]{2,1,0:T(8,128)}, f32[12,96,128]{2,1,0:T(8,128)}, u32[]{:S(2)}, u32[]{:S(2)}) collective-permute-start(f32[12,96,128]{2,1,0:T(8,128)} %get-tuple-element.28.refs_0_), channel_id=1, source_target_pairs={{8,0},{16,8},{24,16},{0,24},{9,1},{17,9},{25,17},{1,25},{10,2},{18... | collective-permute-start | bytes 1769480 | tf_op jit(solution)/shard_map/ppermute | solution.py:647
  56.9 0.7 copy-start.6
  57.6 48.7 %all-to-all-start.2 = ((f32[32,16,128]{2,1,0:T(8,128)}), f32[32,16,128]{2,1,0:T(8,128)S(1)}, u32[]{:S(2)}, u32[]{:S(2)}) async-start(f32[32,16,128]{2,1,0:T(8,128)} %bitcast.6), calls=%async_computation.2 | async-start | bytes 524288 | tf_op jit(solution)/shard_map/all_to_all | solution.py:710

commit v2 on v1

--- a/solution.py
+++ b/solution.py
@@ -18,9 +18,13 @@
 THICK_MAX = 0.017204301
 
 LANES = 128
+BIG = 60
+LATE_MB = 24
+EARLY = 0.01
 HALF = LANES // 2
 PART = LANES // NP
 TYPES = NP - 1
+CHUNKS = (3, 1, 4, 1)
 PARAMS = 6
 VM = pl.BlockSpec(memory_space=pltpu.VMEM)
 ANY = pl.BlockSpec(memory_space=pl.ANY)
@@ -28,12 +32,12 @@
 BF16 = jnp.bfloat16
 
 
-def params(vmem=48):
+def params(vmem=LATE_MB):
     return pltpu.CompilerParams(vmem_limit_bytes=vmem * 1024 * 1024)
 
 
 def cost(us):
-    return pl.CostEstimate(flops=0, bytes_accessed=int(us * 3.0e6), transcendentals=0)
+    return pl.CostEstimate(flops=int(us * 1.0e9), bytes_accessed=int(us * 3.0e6), transcendentals=0)
 
 
 def source_windows(levels):
@@ -157,53 +161,96 @@
     return ref.reshape(lead, LANES)
 
 
-def first_kernel(levels, quad, ndyn, ntrc, dyn4, trc4, thick3, area_ref, m_ref, mw_ref, up_ref, down_ref, edge_ref):
-    dyn, trc, thick = flat(dyn4), flat(trc4), flat(thick3)
+def runs_of(fields):
+    runs = []
+    for source, index in fields:
+        if runs and runs[-1][0] == source and runs[-1][1] + runs[-1][2] == index:
+            runs[-1][2] += 1
+        else:
+            runs.append([source, index, 1])
+    return runs
+
+
+def start_loads(quads, dyn_hbm, trc_hbm, buffer, sems):
+    loads, b, count = [], 0, 0
+    for quad in quads:
+        copies = []
+        for source, index, length in runs_of(quad):
+            ref = dyn_hbm if source == 0 else trc_hbm
+            copies.append(
+                pltpu.make_async_copy(
+                    ref.at[pl.ds(index, length)], buffer.at[pl.ds(b, length)], sems.at[count]
+                )
+            )
+            b, count = b + length, count + 1
+        for copy in copies:
+            copy.start()
+        loads.append(copies)
+    return loads
+
+
+def pack_kernel(levels, chunks, weights_too, dyn_hbm, trc_hbm, thick3, area_ref, m_ref, *rest):
+    buffer, sems = rest[-2:]
+    outs = rest[-2 - 2 * len(chunks) : -2]
+    rest = rest[: -2 - 2 * len(chunks)]
+    quads = [quad for chunk in chunks for quad in chunk]
+    loads = start_loads(quads, dyn_hbm, trc_hbm, buffer, sems)
+    fields, thick = flat(buffer), flat(thick3)
     weight = [area_ref[x : x + 1, :] * thick[pl.ds(x, levels, stride=2), :] for x in range(2)]
     m = m_ref[...]
-    for x, out in ((0, down_ref), (1, up_ref)):
-        packed = pack_quad(dyn, trc, weight, m, quad, x, levels)
-        for kind in range(TYPES):
-            out[kind, 0:levels, :] = packed[:, kind * LANES : (kind + 1) * LANES]
-        out[TYPES, 0:levels, :] = select_dot3(weight[x], mw_ref[...])
-        area = jnp.broadcast_to(area_ref[x : x + 1, :], (8, LANES))
-        out[TYPES, levels : levels + 1, :] = select_dot3(area, mw_ref[...])[0:1]
+    last = TYPES * len(chunks[0])
+    if weights_too:
+        mw_ref = rest[0]
+        for x, out in ((0, outs[1]), (1, outs[0])):
+            out[last, 0:levels, :] = select_dot3(weight[x], mw_ref[...])
+            area = jnp.broadcast_to(area_ref[x : x + 1, :], (8, LANES))
+            out[last, levels : levels + 1, :] = select_dot3(area, mw_ref[...])[0:1]
+    if len(rest) == 4:
+        own_ref, before_ref, after_ref = rest[:3]
+        left = lane_iota(own_ref.shape[1]) < HALF
+        for x, out in ((0, outs[1]), (1, outs[0])):
+            out[last] = own_ref[x] + jnp.where(
+                left, pltpu.roll(before_ref[x], HALF, 1), pltpu.roll(after_ref[x], HALF, 1)
+            )
+    number = 0
+    for place, chunk in enumerate(chunks):
+        for i in range(len(chunk)):
+            for copy in loads[number]:
+                copy.wait()
+            where = [(1, NP * number + b) for b in range(NP)]
+            for x, out in ((0, outs[2 * place + 1]), (1, outs[2 * place])):
+                packed = pack_quad(None, fields, weight, m, where, x, levels)
+                for kind in range(TYPES):
+                    out[TYPES * i + kind, 0:levels, :] = packed[:, kind * LANES : (kind + 1) * LANES]
+            number += 1
+
+
+def ends_kernel(levels, ndyn, ntrc, dyn_hbm, trc_hbm, thick3, area_ref, after_ref, edge_ref, buffer, sems):
+    groups = [[(0, i) for i in range(ndyn)]]
+    groups += [[(1, i) for i in range(k, min(k + 11, ntrc))] for k in range(0, ntrc, 11)]
+    loads = start_loads(groups, dyn_hbm, trc_hbm, buffer, sems)
+    rows, thick = flat(buffer), flat(thick3)
+    weight = [area_ref[x : x + 1, :] * thick[pl.ds(x, levels, stride=2), :] for x in range(2)]
     lane = lane_iota(levels)
     ends = jnp.where(lane < HALF, 0, LANES - 1)
     spot = lane % HALF
-    fields = [(0, i) for i in range(ndyn)] + [(1, i) for i in range(ntrc)]
+    count = ndyn + ntrc
+    totals = [jnp.zeros((levels, LANES), F32)] * 2
+    number = 0
+    for group, copies in zip(groups, loads):
+        for copy in copies:
+            copy.wait()
+        for _ in group:
+            for x in range(2):
+                here = pick_lanes(field_rows(None, rows, levels, (1, number), x), ends)
+                totals[x] = jnp.where(spot == number, here, totals[x])
+            number += 1
     for x in range(2):
-        total = jnp.zeros((levels, LANES), F32)
-        for number, which in enumerate(fields):
-            here = pick_lanes(field_rows(dyn, trc, levels, which, x), ends)
-            total = jnp.where(spot == number, here, total)
         both = pick_lanes(weight[x], ends)
-        total = jnp.where(spot == len(fields), 1.0, total) * both
-        edge_ref[x, 0:levels, :] = total
+        edge_ref[x, 0:levels, :] = jnp.where(spot == count, 1.0, totals[x]) * both
         edge_ref[x, levels : levels + 1, :] = pick_lanes(
             jnp.broadcast_to(area_ref[x : x + 1, :], (8, LANES)), ends[0:8]
         )[0:1]
-
-
-def pack_kernel(levels, chunks, dyn4, trc4, thick3, area_ref, m_ref, *outs):
-    dyn, trc, thick = flat(dyn4), flat(trc4), flat(thick3)
-    weight = [area_ref[x : x + 1, :] * thick[pl.ds(x, levels, stride=2), :] for x in range(2)]
-    m = m_ref[...]
-    for number, quads in enumerate(chunks):
-        up_ref, down_ref = outs[2 * number], outs[2 * number + 1]
-        for i, quad in enumerate(quads):
-            for x, out in ((0, down_ref), (1, up_ref)):
-                packed = pack_quad(dyn, trc, weight, m, quad, x, levels)
-                for kind in range(TYPES):
-                    out[TYPES * i + kind, 0:levels, :] = packed[:, kind * LANES : (kind + 1) * LANES]
-
-
-def edge_kernel(own_ref, before_ref, after_ref, row0_ref, row1_ref):
-    left = lane_iota(own_ref.shape[1]) < HALF
-    for x, out in ((0, row0_ref), (1, row1_ref)):
-        out[...] = own_ref[x] + jnp.where(
-            left, pltpu.roll(before_ref[x], HALF, 1), pltpu.roll(after_ref[x], HALF, 1)
-        )
 
 
 def remap_group(levels, windows, summed, rm, thick, al, ar, aq, rdt, tile_of, row_of, s_ref):
@@ -257,7 +304,7 @@
 
 def setup_kernel(levels, nfields, own0, own1, from_up, from_down, row0, row1, edge_up, edge_down, p_ref, i_ref, e_ref, surface_ref, s_ref):
     windows = tile_windows(levels)
-    rows = row0.shape[0]
+    rows = row0.shape[1]
     tiles = rows // 8
     row = row_iota(rows)
     lane = lane_iota(rows)
@@ -269,9 +316,9 @@
         own, got = ((own0, from_up), (own1, from_down))[x]
         eown, egot = ((row0, edge_up), (row1, edge_down))[x]
         if base < 2:
-            mass = own[TYPES] + got[TYPES]
+            mass = own[0] + got[0]
         else:
-            summed = eown[...] + egot[...]
+            summed = eown[0] + egot[0]
             mass = pick_lanes(summed, edge_lanes)
         area = mass[levels : levels + 1]
         mass = jnp.where(inside, mass, 1.0)
@@ -334,9 +381,9 @@
             )[0:1]
 
 
-def remap_kernel(levels, quads, aliased, own0, own1, from_up, from_down, p_ref, i_ref, e_ref, mt_ref, *rest):
+def remap_kernel(levels, ndyn, quads, aliased, extra, own0, own1, from_up, from_down, p_ref, i_ref, e_ref, mt_ref, *rest):
     if aliased:
-        rest = rest[2:]
+        rest = rest[2 + extra :]
         dyn_ref, trc_ref = rest[:2]
         columns_ref = None
         rest = rest[2:]
@@ -351,13 +398,6 @@
     half = jnp.where(lane < HALF, 0, HALF)
     out_rows = flat(out_ref)
     fields = TYPES + 1
-
-    ndyn = sum(1 for which in sum(quads, []) if which[0] == 0)
-
-    def numbers(i, b):
-        source, index = quads[0][b]
-        first = index + (0 if source == 0 else 3)
-        return first
 
     def one_quad(i, edge_lane):
         for kind in range(TYPES):
@@ -376,33 +416,21 @@
                 outer = pick_lanes(e_ref[x, 0:levels, :], half + edge_lane(b))
                 value = jnp.where(ends, outer, value)
                 out_rows[pl.ds((i * fields + b) * 2 * levels + x, levels, stride=2), :] = value
-                if columns_ref is not None:
+                if columns_ref is not None and isinstance(i, int) and i == 0:
                     columns_ref[b, 0:levels, x * LANES : (x + 1) * LANES] = value
 
-    table = [[index + (0 if source == 0 else 3) for source, index in quad] for quad in quads]
+    table = [[index + (0 if source == 0 else ndyn) for source, index in quad] for quad in quads]
+    start = len(quads) - 1 if aliased else max(len(quads) - 1, 1)
+    while start > 1 and table[start] == [v + fields for v in table[start - 1]]:
+        start -= 1
+    for i in range(start):
+        one_quad(i, lambda b: table[i][b])
+
+    @pl.loop(start, len(quads))
+    def _(i):
+        one_quad(i, lambda b: table[start][b] + fields * (i - start))
+
     copies = []
-    for i, quad in enumerate(quads):
-        if i == 0 or len(quads) == 1:
-            pass
-    if len(quads) == 1:
-        one_quad(0, lambda b: table[0][b])
-    else:
-        steps = [table[i][b] - 4 * i for i in range(len(quads)) for b in range(fields)]
-        base = table[0]
-        regular = all(table[i][b] == base[b] + 4 * i for i in range(len(quads)) for b in range(fields))
-        if regular:
-
-            @pl.loop(0, len(quads))
-            def _(i):
-                one_quad(i, lambda b: base[b] + 4 * i)
-        else:
-            one_quad(0, lambda b: table[0][b])
-            later = table[1]
-
-            @pl.loop(1, len(quads))
-            def _(i):
-                one_quad(i, lambda b: later[b] + 4 * (i - 1))
-
     for i, quad in enumerate(quads):
         b = 0
         while b < fields:
@@ -494,7 +522,8 @@
     return jnp.concatenate([x, jnp.zeros((LANES - x.shape[0], x.shape[1]), x.dtype)], 0)
 
 
-def cloud_kernel(devices, counts_ref, cloud_ref, send_ref):
+def cloud_kernel(devices, counts_ref, cloud_ref, *rest):
+    send_ref = rest[-1]
     hot = slot_rows(devices, counts_ref, cloud_ref.shape[1])
     send_ref[...] = to_slots(hot, pad_rows(cloud_ref[...]))
 
@@ -573,98 +602,120 @@
     fields = [(0, i) for i in range(1, ndyn)] + [(1, i) for i in range(3, ntrc)]
     quads = [fields[i : i + 4] for i in range(0, len(fields), 4)]
     first_quad = [(0, 0), (1, 0), (1, 1), (1, 2)]
-    chunks = [quads[:4], quads[4:]]
+    quads = [first_quad] + quads
+    chunks, begin = [], 0
+    for length in CHUNKS:
+        chunks.append(quads[begin : begin + length])
+        begin += length
+    assert begin == len(quads)
     matrix = pack_matrix()
     m = jnp.asarray(matrix, BF16)
     mt = jnp.asarray(matrix.T, BF16)
     mw = jnp.asarray(weight_matrix(), BF16)
     up, down = ring("gx")
     right, left = ring("gy")
+    fields_in = (dynamics, tracers, thickness, area_weight)
+
+    packed, received = [None] * len(chunks), [None] * len(chunks)
+
+    def send(numbers, extra, args, specs, name):
+        parts = [chunks[n] for n in numbers]
+        total = sum(len(part) for part in parts)
+        sent = pl.pallas_call(
+            lambda *refs: pack_kernel(levels, parts, numbers[0] == 0, *refs),
+            out_shape=tuple(
+                shape(TYPES * len(part) + extra, rows, LANES) for part in parts for _ in range(2)
+            ),
+            in_specs=[ANY, ANY] + [VM] * 3 + specs,
+            out_specs=(VM,) * (2 * len(parts)),
+            scratch_shapes=[
+                pltpu.VMEM((NP * total, levels, 2, LANES), F32),
+                pltpu.SemaphoreType.DMA((2 * total,)),
+            ],
+            compiler_params=params(BIG),
+            cost_estimate=cost(EARLY),
+            name=name,
+        )(*fields_in, m, *args)
+        for i, n in enumerate(numbers):
+            packed[n] = (sent[2 * i], sent[2 * i + 1])
+            received[n] = (
+                lax.ppermute(sent[2 * i], "gx", up),
+                lax.ppermute(sent[2 * i + 1], "gx", down),
+            )
 
     counts, position = pl.pallas_call(
         lambda *refs: route_kernel(devices, *refs),
         out_shape=(shape(devices, 1, LANES), shape(1, columns, dtype=jnp.int32)),
         in_specs=[VM],
         out_specs=(VM, VM),
-        compiler_params=params(),
-        cost_estimate=cost(1),
+        compiler_params=params(BIG),
+        cost_estimate=cost(EARLY),
         name="route",
     )(owner)
     counts_in = lax.all_to_all(counts, axes, split_axis=0, concat_axis=0, tiled=True)
 
-    up0, down0, edges = pl.pallas_call(
-        lambda *refs: first_kernel(levels, first_quad, ndyn, ntrc, *refs),
-        out_shape=(shape(TYPES + 1, rows, LANES),) * 2 + (shape(2, rows, LANES),),
-        in_specs=[VM] * 6,
-        out_specs=(VM,) * 3,
-        compiler_params=params(),
-        cost_estimate=cost(4),
-        name="first_pack",
-    )(dynamics, tracers, thickness, area_weight, m, mw)
+    send([0], 1, (mw, counts), [VM, ANY], "first_pack")
+
+    edges = pl.pallas_call(
+        lambda *refs: ends_kernel(levels, ndyn, ntrc, *refs),
+        out_shape=shape(2, rows, LANES),
+        in_specs=[ANY, ANY, VM, VM, ANY],
+        out_specs=VM,
+        scratch_shapes=[
+            pltpu.VMEM((nfields, levels, 2, LANES), F32),
+            pltpu.SemaphoreType.DMA((8,)),
+        ],
+        compiler_params=params(BIG),
+        cost_estimate=cost(EARLY),
+        name="ends",
+    )(*fields_in, packed[0][0])
     before = lax.ppermute(edges, "gy", right)
     after = lax.ppermute(edges, "gy", left)
-    from_up0 = lax.ppermute(up0, "gx", up)
-    from_down0 = lax.ppermute(down0, "gx", down)
-
-    packed = pl.pallas_call(
-        lambda *refs: pack_kernel(levels, chunks, *refs),
-        out_shape=tuple(shape(TYPES * len(c), rows, LANES) for c in chunks for _ in range(2)),
-        in_specs=[VM] * 5,
-        out_specs=(VM,) * (2 * len(chunks)),
-        compiler_params=params(),
-        cost_estimate=cost(6),
-        name="pack",
-    )(dynamics, tracers, thickness, area_weight, m)
-
-    row0, row1 = pl.pallas_call(
-        edge_kernel,
-        out_shape=(shape(rows, LANES),) * 2,
-        in_specs=[VM] * 3,
-        out_specs=(VM,) * 2,
-        compiler_params=params(),
-        cost_estimate=cost(1),
-        name="edge_sum",
-    )(edges, before, after)
-    edge_up = lax.ppermute(row1, "gx", up)
-    edge_down = lax.ppermute(row0, "gx", down)
 
     cloud_out = pl.pallas_call(
         lambda *refs: cloud_kernel(devices, *refs),
         out_shape=shape(slots, LANES),
-        in_specs=[VM] * 2,
+        in_specs=[VM] * 2 + [ANY] * 3,
         out_specs=VM,
         compiler_params=params(),
         cost_estimate=cost(2),
         name="cloud_send",
-    )(counts_in, cloud_frac)
+    )(counts_in, cloud_frac, packed[0][0], *received[0])
     cloud_in = lax.all_to_all(cloud_out, axes, split_axis=0, concat_axis=0, tiled=True)
 
-    received = []
-    for number in range(len(chunks)):
-        received.append(
-            (
-                lax.ppermute(packed[2 * number], "gx", up),
-                lax.ppermute(packed[2 * number + 1], "gx", down),
-            )
-        )
+    send([1], 1, (edges, before, after, cloud_out), [VM] * 3 + [ANY], "second_pack")
+
+    send(list(range(2, len(chunks))), 0, (packed[1][0],), [ANY], "pack")
+    def one_group(number):
+        group = TYPES * len(chunks[number])
+        return pl.BlockSpec((1, rows, LANES), lambda i: (group, 0, 0))
+
+    def full(*dims):
+        return pl.BlockSpec(dims, lambda i: (0,) * len(dims))
 
     weights, indices, edge_values, surface = pl.pallas_call(
         lambda *refs: setup_kernel(levels, nfields, *refs),
+        grid=(1,),
         out_shape=(
             shape(2 * TYPES, PARAMS, rows, LANES),
             shape(2 * TYPES, 2, rows, LANES, dtype=jnp.int32),
             shape(2, rows, LANES),
             shape(1, columns),
         ),
-        in_specs=[VM] * 8,
-        out_specs=(VM,) * 4,
+        in_specs=[one_group(0)] * 4 + [one_group(1)] * 4,
+        out_specs=(
+            full(2 * TYPES, PARAMS, rows, LANES),
+            full(2 * TYPES, 2, rows, LANES),
+            full(2, rows, LANES),
+            full(1, columns),
+        ),
         scratch_shapes=[pltpu.VMEM((3, rows + 16, LANES), F32)],
-        compiler_params=params(),
+        compiler_params=params(BIG),
         cost_estimate=cost(5),
         name="column_setup",
-    )(down0, up0, from_up0, from_down0, row0, row1, edge_up, edge_down)
-
-    def remap(chunk, own0, own1, got_up, got_down, so_far):
+    )(packed[0][1], packed[0][0], *received[0], packed[1][1], packed[1][0], *received[1])
+
+    def remap(chunk, own0, own1, got_up, got_down, so_far, follows=()):
         aliased = so_far is not None
         out_shape = (shape(*dynamics.shape), shape(*tracers.shape))
         args = [own0, own1, got_up, got_down, weights, indices, edge_values, mt]
@@ -672,14 +723,14 @@
         out_specs = (ANY, ANY)
         aliases = {}
         if aliased:
-            args += list(so_far)
-            in_specs += [ANY, ANY]
+            args += list(so_far) + list(follows)
+            in_specs += [ANY] * (2 + len(follows))
             aliases = {8: 0, 9: 1}
         else:
             out_shape += (shape(4, rows, columns),)
             out_specs += (VM,)
         return pl.pallas_call(
-            lambda *refs: remap_kernel(levels, chunk, aliased, *refs),
+            lambda *refs: remap_kernel(levels, ndyn, chunk, aliased, len(follows), *refs),
             out_shape=out_shape,
             in_specs=in_specs,
             out_specs=out_specs,
@@ -691,11 +742,13 @@
                 pltpu.SemaphoreType.DMA((2 * len(chunk),)),
             ],
             compiler_params=params(),
-            cost_estimate=cost(4 * len(chunk)),
+            cost_estimate=cost(2 * len(chunk)),
             name="remap",
         )(*args)
 
-    dyn_new, trc_new, physics_columns = remap([first_quad], down0, up0, from_up0, from_down0, None)
+    dyn_new, trc_new, physics_columns = remap(
+        chunks[0], packed[0][1], packed[0][0], *received[0], None
+    )
 
     increments, next_out = pl.pallas_call(
         lambda *refs: physics_kernel(levels, *refs),
@@ -710,8 +763,8 @@
     next_in = lax.all_to_all(next_out, axes, split_axis=0, concat_axis=0, tiled=True)
 
     done = (dyn_new, trc_new)
-    for number, chunk in enumerate(chunks):
-        done = remap(chunk, packed[2 * number + 1], packed[2 * number], *received[number], done)
+    for number, chunk in list(enumerate(chunks))[1:]:
+        done = remap(chunk, packed[number][1], packed[number][0], *received[number], done, (next_out,) if number > 1 else ())
 
     cloud_next = pl.pallas_call(
         lambda *refs: final_kernel(devices, levels, *refs),

time: 108 us -> 98.3 us (0.910)
  waiting for transfers between devices: 30.2 us -> 14.1 us
  blocking collectives: 14.3 us -> 0 us
  Pallas kernels: 30.4 us -> 42.3 us
  starting transfers between devices: 23.4 us -> 29.4 us
  local copies, waits for them, and re-layouts: 8.48 us -> 10.7 us
    ppermute x8, waiting for transfers between devices: 30.1 us -> 0.91 us  [the longest x4 0.9 us: send(): lax.ppermute(sent[2 * i + 1], 'gx', down)]
    all_to_all x1 -> x0, blocking collectives: 14.3 us -> none  [local(): lax.all_to_all(counts, axes, split_axis=0, concat_axis=0, tiled=True)]
    all_to_all x0 -> x1, waiting for transfers between devices: none -> 13.2 us  [local(): lax.all_to_all(counts, axes, split_axis=0, concat_axis=0, tiled=True)]
    pallas_call x7 -> x9, Pallas kernels: 26.4 us -> 36.7 us  [the longest x4 15.6 us: remap(): pl.pallas_call(lambda *refs: remap_kernel(levels, ndyn, chunk, aliased, l...]
    all_to_all x0 -> x1, starting transfers between devices: none -> 4.21 us  [local(): lax.all_to_all(counts, axes, split_axis=0, concat_axis=0, tiled=True)]
    unnamed x26 -> x66, local copies, waits for them, and re-layouts: 8.48 us -> 10.7 us
    ppermute x8, starting transfers between devices: 15.4 us -> 17 us  [the longest x4 11.5 us: send(): lax.ppermute(sent[2 * i + 1], 'gx', down)]
    pallas_call x1, Pallas kernels: 0.14 us -> 1.43 us  [local(): pl.pallas_call(lambda *refs: route_kernel(devices, *refs), out_shape=(sha...]
  transfers between devices with their start and end apart: 12 -> 13, of which waited for: 5 -> 2; matrix products, arithmetic and copies ran while one was open for 0% -> 0% of each run, Pallas kernels for 26% -> 33%
where the time goes in v2:
time: 98.3 us; the launch traced here: 97.5 us
  Pallas kernels  42.3 us (43%)
  starting transfers between devices  29.4 us (30%)
  waiting for transfers between devices  14.1 us (14%)
  local copies, waits for them, and re-layouts  10.7 us (11%)
  between operations  1.02 us (1%)
    pallas_call x4, Pallas kernels, remap(): pl.pallas_call(lambda *refs: remap_kernel(levels, ndyn, chunk, aliased, l...  15.6 us
    all_to_all x1, waiting for transfers between devices, local(): lax.all_to_all(counts, axes, split_axis=0, concat_axis=0, tiled=True)  13.2 us
    pallas_call x3, Pallas kernels, send(): pl.pallas_call(lambda *refs: pack_kernel(levels, parts, numbers[0] == 0,...  12.5 us
    ppermute x4, starting transfers between devices, send(): lax.ppermute(sent[2 * i + 1], 'gx', down)  11.5 us
    unnamed x66, local copies, waits for them, and re-layouts  10.7 us
    ppermute x4, starting transfers between devices, send(): lax.ppermute(sent[2 * i], 'gx', up)  5.43 us
    pallas_call x1, Pallas kernels, local(): pl.pallas_call(lambda *refs: setup_kernel(levels, nfields, *refs), grid=(...  4.52 us
    all_to_all x1, starting transfers between devices, local(): lax.all_to_all(counts, axes, split_axis=0, concat_axis=0, tiled=True)  4.21 us
  transfers between devices with their start and end apart: 13, of which 2 were waited for; matrix products, arithmetic and copies ran while one was open for 0% of the time, Pallas kernels for 33%

profile of v2, /device:TPU:0, one launch (start us, length us, event | category | flops | bytes accessed | tf_op | source)
XLA Modules:
  0.0 97.5 jit_solution(8031634285114391563)
XLA Ops:
  0.6 1.4 %route.1 = (f32[32,1,128]{2,1,0:T(1,128)}, s32[1,256]{1,0:T(1,128)}) custom-call(s32[2,128]{1,0:T(2,128)} %refs_0_.5), custom_call_target="tpu_custom_call" | custom-call | flops 10000000 | bytes 30000 | tf_op jit(solution)/shard_map/route/pallas_call | solution.py:646
  2.1 4.3 %first_pack.1 = (f32[10,96,128]{2,1,0:T(8,128)}, f32[10,96,128]{2,1,0:T(8,128)}) custom-call(f32[3,93,2,128]{3,2,1,0:T(2,128)} %refs_0_.9, f32[33,93,2,128]{3,2,1,0:T(2,128)} %refs_1_.9, f32[93,2,128]{2,1,0:T(2,128)} %refs_2_.7, f32[2,128]{1,0:T(2,128)} %refs_3_.7, bf16[512,384]{1,0:T(8,128)(2,1)} %constant.6.clone.refs_4_, ...), custom_call_target="tpu_custom_call" | custom-call | flops 10000000 | bytes 30000 | tf_op jit(solution)/shard_map/first_pack/pallas_call | solution.py:624
  6.3 3.1 %collective-permute-start.2 = (f32[10,96,128]{2,1,0:T(8,128)}, f32[10,96,128]{2,1,0:T(8,128)S(1)}, u32[]{:S(2)}, u32[]{:S(2)}) collective-permute-start(f32[10,96,128]{2,1,0:T(8,128)} %get-tuple-element.30.refs_4_.refs_2_.refs_1_), channel_id=1, source_target_pairs={{0,8},{8,16},{16,24},{24,0},{1,9},{9,17},{17,25},{25,1},{2,10},{10... | collective-permute-start | bytes 1474568 | tf_op jit(solution)/shard_map/ppermute | solution.py:642
  9.4 2.1 %collective-permute-start.3 = (f32[10,96,128]{2,1,0:T(8,128)}, f32[10,96,128]{2,1,0:T(8,128)S(1)}, u32[]{:S(2)}, u32[]{:S(2)}) collective-permute-start(f32[10,96,128]{2,1,0:T(8,128)} %get-tuple-element.31.refs_0_), channel_id=1, source_target_pairs={{8,0},{16,8},{24,16},{0,24},{9,1},{17,9},{25,17},{1,25},{10,2},{18... | collective-permute-start | bytes 1474568 | tf_op jit(solution)/shard_map/ppermute | solution.py:643
  11.5 4.2 %all-to-all-start = ((f32[32,1,128]{2,1,0:T(1,128)}), f32[32,1,128]{2,1,0:T(1,128)S(1)}, u32[]{:S(2)}, u32[]{:S(2)}) async-start(f32[32,1,128]{2,1,0:T(1,128)} %get-tuple-element.29.refs_6_), calls=%async_computation | async-start | bytes 32768 | tf_op jit(solution)/shard_map/all_to_all | solution.py:655
  15.7 4.0 %ends.1.refs_5_ = f32[2,96,128]{2,1,0:T(8,128)} custom-call(f32[3,93,2,128]{3,2,1,0:T(2,128)} %refs_0_.9, f32[33,93,2,128]{3,2,1,0:T(2,128)} %refs_1_.9, f32[93,2,128]{2,1,0:T(2,128)} %refs_2_.7, f32[2,128]{1,0:T(2,128)} %refs_3_.7, f32[10,96,128]{2,1,0:T(8,128)} %get-tuple-element.30.refs_4_.refs_2_.refs_1_), custom_call_target="tpu_custom_call" | custom-call | flops 10000000 | bytes 30000 | tf_op jit(solution)/shard_map/ends/pallas_call | solution.py:659
  20.0 2.4 %collective-permute-start.1 = (f32[2,96,128]{2,1,0:T(8,128)}, f32[2,96,128]{2,1,0:T(8,128)S(1)}, u32[]{:S(2)}, u32[]{:S(2)}) collective-permute-start(f32[2,96,128]{2,1,0:T(8,128)} %ends.1.refs_5_), channel_id=1, source_target_pairs={{1,0},{2,1},{3,2},{4,3},{5,4},{6,5},{7,6},{0,7},{9,8},{10,9},{11,1... | collective-permute-start | bytes 294920 | tf_op jit(solution)/shard_map/ppermute | solution.py:673
  22.4 13.2 %all-to-all-done.refs_0_ = f32[32,1,128]{2,1,0:T(1,128)S(1)} async-done(((f32[32,1,128]{2,1,0:T(1,128)}), f32[32,1,128]{2,1,0:T(1,128)S(1)}, u32[]{:S(2)}, u32[]{:S(2)}) %all-to-all-start) | async-done | bytes 16416 | tf_op jit(solution)/shard_map/all_to_all | solution.py:655
  35.6 1.2 %cloud_send.1.refs_8_ = f32[512,128]{1,0:T(8,128)} custom-call(f32[32,1,128]{2,1,0:T(1,128)S(1)} %all-to-all-done.refs_0_, f32[93,256]{1,0:T(8,128)S(1)} %copy-done.17, f32[10,96,128]{2,1,0:T(8,128)S(1)} %copy-done, f32[10,96,128]{2,1,0:T(8,128)S(1)} %collective-permute-done.2.refs_3_.refs_2_, f32[10,96,128]{2,1,0:T(8,128)S(1)} %collective-permute-done.3.refs_4_.refs_3_), custom_call_target="tpu_custom_call" | custom-call | flops 2000000000 | bytes 6000000 | tf_op jit(solution)/shard_map/cloud_send/pallas_call | solution.py:675
  38.2 3.3 %second_pack.1 = (f32[4,96,128]{2,1,0:T(8,128)}, f32[4,96,128]{2,1,0:T(8,128)}) custom-call(f32[3,93,2,128]{3,2,1,0:T(2,128)} %refs_0_.9, f32[33,93,2,128]{3,2,1,0:T(2,128)} %refs_1_.9, f32[93,2,128]{2,1,0:T(2,128)} %refs_2_.7, f32[2,128]{1,0:T(2,128)} %refs_3_.7, bf16[512,384]{1,0:T(8,128)(2,1)} %constant.6.clone.refs_4_, f32[2,96,128]{2,1,0:T(8,128)} %ends.1.refs_5_, ...), custom_call_target="tpu_custom_call" | custom-call | flops 10000000 | bytes 30000 | tf_op jit(solution)/shard_map/second_pack/pallas_call | solution.py:624
  42.1 3.2 %collective-permute-start.7 = (f32[4,96,128]{2,1,0:T(8,128)}, f32[4,96,128]{2,1,0:T(8,128)S(1)}, u32[]{:S(2)}, u32[]{:S(2)}) collective-permute-start(f32[4,96,128]{2,1,0:T(8,128)} %get-tuple-element.35.refs_4_.refs_0_), channel_id=1, source_target_pairs={{8,0},{16,8},{24,16},{0,24},{9,1},{17,9},{25,17},{1,25},{10,2},{18... | collective-permute-start | bytes 589832 | tf_op jit(solution)/shard_map/ppermute | solution.py:643
  45.3 2.6 %all-to-all-start.1 = ((f32[32,16,128]{2,1,0:T(8,128)}), f32[32,16,128]{2,1,0:T(8,128)S(1)}, u32[]{:S(2)}, u32[]{:S(2)}) async-start(f32[32,16,128]{2,1,0:T(8,128)} %bitcast), calls=%async_computation.1 | async-start | bytes 524288 | tf_op jit(solution)/shard_map/all_to_all | solution.py:684
  47.9 5.0 %pack.1 = (f32[12,96,128]{2,1,0:T(8,128)}, f32[12,96,128]{2,1,0:T(8,128)}, f32[3,96,128]{2,1,0:T(8,128)}, f32[3,96,128]{2,1,0:T(8,128)}) custom-call(f32[3,93,2,128]{3,2,1,0:T(2,128)} %refs_0_.9, f32[33,93,2,128]{3,2,1,0:T(2,128)} %refs_1_.9, f32[93,2,128]{2,1,0:T(2,128)} %refs_2_.7, f32[2,128]{1,0:T(2,128)} %refs_3_.7, ...), custom_call_target="tpu_custom_call" | custom-call | flops 10000000 | bytes 30000 | tf_op jit(solution)/shard_map/pack/pallas_call | solution.py:624
  52.9 1.7 %collective-permute-start.8 = (f32[12,96,128]{2,1,0:T(8,128)}, f32[12,96,128]{2,1,0:T(8,128)S(1)}, u32[]{:S(2)}, u32[]{:S(2)}) collective-permute-start(f32[12,96,128]{2,1,0:T(8,128)} %get-tuple-element.40.refs_1_), channel_id=1, source_target_pairs={{0,8},{8,16},{16,24},{24,0},{1,9},{9,17},{17,25},{25,1},{2,10},{10... | collective-permute-start | bytes 1769480 | tf_op jit(solution)/shard_map/ppermute | solution.py:642
  54.7 2.1 %collective-permute-start.9 = (f32[12,96,128]{2,1,0:T(8,128)}, f32[12,96,128]{2,1,0:T(8,128)S(1)}, u32[]{:S(2)}, u32[]{:S(2)}) collective-permute-start(f32[12,96,128]{2,1,0:T(8,128)} %get-tuple-element.39.refs_0_), channel_id=1, source_target_pairs={{8,0},{16,8},{24,16},{0,24},{9,1},{17,9},{25,17},{1,25},{10,2},{18... | collective-permute-start | bytes 1769480 | tf_op jit(solution)/shard_map/ppermute | solution.py:643
  56.9 4.0 %collective-permute-start.5 = (f32[3,96,128]{2,1,0:T(8,128)}, f32[3,96,128]{2,1,0:T(8,128)}, u32[]{:S(2)}, u32[]{:S(2)}) collective-permute-start(f32[3,96,128]{2,1,0:T(8,128)} %get-tuple-element.33.refs_0_), channel_id=1, source_target_pairs={{8,0},{16,8},{24,16},{0,24},{9,1},{17,9},{25,17},{1,25},{10,2},{18... | collective-permute-start | bytes 442376 | tf_op jit(solution)/shard_map/ppermute | solution.py:643
  61.6 4.5 %column_setup.1 = (f32[6,6,96,128]{3,2,1,0:T(8,128)}, s32[6,2,96,128]{3,2,1,0:T(8,128)}, f32[2,96,128]{2,1,0:T(8,128)}, f32[1,256]{1,0:T(1,128)}) custom-call(f32[10,96,128]{2,1,0:T(8,128)} %get-tuple-element.31.refs_0_, f32[10,96,128]{2,1,0:T(8,128)} %get-tuple-element.30.refs_4_.refs_2_.refs_1_, f32[10,96,128]{2,1,0:T(8,128)} %copy-done.6, ...), custom_call_target="tpu_custom_call" | custom-call | flops 5000000000 | bytes 15000000 | tf_op jit(solution)/shard_map/column_setup/pallas_call | solution.py:696
  66.1 1.0 %copy-done.19 = bf16[384,512]{1,0:T(8,128)(2,1)S(1)} copy-done((bf16[384,512]{1,0:T(8,128)(2,1)S(1)}, bf16[384,512]{1,0:T(8,128)(2,1)}, u32[]{:S(2)}) %copy-start.19) | copy-done | bytes 393240
  67.1 1.5 %copy-done.21 = f32[6,6,96,128]{3,2,1,0:T(8,128)S(1)} copy-done((f32[6,6,96,128]{3,2,1,0:T(8,128)S(1)}, f32[6,6,96,128]{3,2,1,0:T(8,128)}, u32[]{:S(2)}) %copy-start.21) | copy-done | bytes 1769496
  68.6 1.1 %copy-done.23 = s32[6,2,96,128]{3,2,1,0:T(8,128)S(1)} copy-done((s32[6,2,96,128]{3,2,1,0:T(8,128)S(1)}, s32[6,2,96,128]{3,2,1,0:T(8,128)}, u32[]{:S(2)}) %copy-start.23) | copy-done | bytes 589848
  69.7 0.9 copy-done.25
  70.6 4.3 %remap.4 = (f32[3,93,2,128]{3,2,1,0:T(2,128)}, f32[33,93,2,128]{3,2,1,0:T(2,128)}, f32[4,96,256]{2,1,0:T(8,128)S(1)}) custom-call(f32[10,96,128]{2,1,0:T(8,128)S(1)} %copy-done.5, f32[10,96,128]{2,1,0:T(8,128)S(1)} %copy-done.1, f32[10,96,128]{2,1,0:T(8,128)S(1)} %copy-done.7, f32[10,96,128]{2,1,0:T(8,128)S(1)} %copy-done.9, ...), custom_call_target="tpu_custom_call" | custom-call | flops 6000000000 | bytes 18000000 | tf_op jit(solution)/shard_map/remap/pallas_call | solution.py:732
  75.7 2.0 %remap.5 = (f32[3,93,2,128]{3,2,1,0:T(2,128)}, f32[33,93,2,128]{3,2,1,0:T(2,128)}) custom-call(f32[4,96,128]{2,1,0:T(8,128)S(1)} %copy-done.10, f32[4,96,128]{2,1,0:T(8,128)S(1)} %copy-done.2, f32[4,96,128]{2,1,0:T(8,128)S(1)} %copy-done.12, f32[4,96,128]{2,1,0:T(8,128)S(1)} %copy-done.14, ...), custom_call_target="tpu_custom_call", output_to_operand_aliasing={{0}: (8, {}), {1}: (9, {})} | custom-call | flops 2000000000 | bytes 6000000 | tf_op jit(solution)/shard_map/remap/pallas_call | solution.py:732
  77.8 1.0 %copy-done.29 = f32[4,96,256]{2,1,0:T(8,128)S(1)} copy-done((f32[4,96,256]{2,1,0:T(8,128)S(1)}, f32[4,96,256]{2,1,0:T(8,128)}, u32[]{:S(2)}) %copy-start.29) | copy-done | bytes 393240
  78.8 1.8 %physics.1 = (f32[4,93,2,128]{3,2,1,0:T(2,128)}, f32[512,128]{1,0:T(8,128)}) custom-call(f32[4,96,256]{2,1,0:T(8,128)S(1)} %copy-done.29, f32[512,128]{1,0:T(8,128)S(1)} %bitcast.4, s32[1,256]{1,0:T(1,128)S(1)} %copy-done.27, f32[1,256]{1,0:T(1,128)S(1)} %copy-done.30, s32[2,128]{1,0:T(2,128)S(1)} %copy-done.18), custom_call_target="tpu_custom_call" | custom-call | flops 5000000000 | bytes 15000000 | tf_op jit(solution)/shard_map/physics/pallas_call | solution.py:753
  80.6 2.9 %all-to-all-start.2 = ((f32[32,16,128]{2,1,0:T(8,128)}), f32[32,16,128]{2,1,0:T(8,128)S(1)}, u32[]{:S(2)}, u32[]{:S(2)}) async-start(f32[32,16,128]{2,1,0:T(8,128)} %bitcast.2), calls=%async_computation.2 | async-start | bytes 524288 | tf_op jit(solution)/shard_map/all_to_all | solution.py:763
  83.5 0.9 collective-permute-done.9.refs_3_
  84.4 1.5 %copy-done.22 = f32[6,6,96,128]{3,2,1,0:T(8,128)S(1)} copy-done((f32[6,6,96,128]{3,2,1,0:T(8,128)S(1)}, f32[6,6,96,128]{3,2,1,0:T(8,128)}, u32[]{:S(2)}) %copy-start.22) | copy-done | bytes 1769496
  85.9 1.1 %copy-done.24 = s32[6,2,96,128]{3,2,1,0:T(8,128)S(1)} copy-done((s32[6,2,96,128]{3,2,1,0:T(8,128)S(1)}, s32[6,2,96,128]{3,2,1,0:T(8,128)}, u32[]{:S(2)}) %copy-start.24) | copy-done | bytes 589848
  86.9 6.3 %remap.6 = (f32[3,93,2,128]{3,2,1,0:T(2,128)}, f32[33,93,2,128]{3,2,1,0:T(2,128)}) custom-call(f32[12,96,128]{2,1,0:T(8,128)S(1)} %copy-done.4, f32[12,96,128]{2,1,0:T(8,128)S(1)} %copy-done.3, f32[12,96,128]{2,1,0:T(8,128)S(1)} %collective-permute-done.8.refs_2_, ...), custom_call_target="tpu_custom_call", output_to_operand_aliasing={{0}: (8, {}), {1}: (9, {})} | custom-call | flops 8000000000 | bytes 24000000 | tf_op jit(solution)/shard_map/remap/pallas_call | solution.py:732
  93.3 3.0 %remap.7 = (f32[3,93,2,128]{3,2,1,0:T(2,128)}, f32[33,93,2,128]{3,2,1,0:T(2,128)}) custom-call(f32[3,96,128]{2,1,0:T(8,128)S(1)} %copy-done.16, f32[3,96,128]{2,1,0:T(8,128)S(1)} %copy-done.15, f32[3,96,128]{2,1,0:T(8,128)S(1)} %collective-permute-done.4.refs_2_, ...), custom_call_target="tpu_custom_call", output_to_operand_aliasing={{0}: (8, {}), {1}: (9, {})} | custom-call | flops 2000000000 | bytes 6000000 | tf_op jit(solution)/shard_map/remap/pallas_call | solution.py:732
  96.3 1.2 %cloud_receive.1 = f32[93,256]{1,0:T(8,128)} custom-call(f32[32,1,128]{2,1,0:T(1,128)S(1)} %all-to-all-done.refs_0_, f32[512,128]{1,0:T(8,128)S(1)} %bitcast.5), custom_call_target="tpu_custom_call" | custom-call | flops 2000000000 | bytes 6000000 | tf_op jit(solution)/shard_map/cloud_receive/pallas_call | solution.py:769
  (73 shorter events, 3.8 us)
Async XLA Ops:
  2.1 33.5 %copy-start.17 = (f32[93,256]{1,0:T(8,128)S(1)}, f32[93,256]{1,0:T(8,128)}, u32[]{:S(2)}) copy-start(f32[93,256]{1,0:T(8,128)} %refs_1_.7) | copy-start | bytes 285700
  6.3 29.3 %copy-start = (f32[10,96,128]{2,1,0:T(8,128)S(1)}, f32[10,96,128]{2,1,0:T(8,128)}, u32[]{:S(2)}) copy-start(f32[10,96,128]{2,1,0:T(8,128)} %get-tuple-element.30.refs_4_.refs_2_.refs_1_) | copy-start | bytes 1474564
  6.3 29.2 %collective-permute-start.2 = (f32[10,96,128]{2,1,0:T(8,128)}, f32[10,96,128]{2,1,0:T(8,128)S(1)}, u32[]{:S(2)}, u32[]{:S(2)}) collective-permute-start(f32[10,96,128]{2,1,0:T(8,128)} %get-tuple-element.30.refs_4_.refs_2_.refs_1_), channel_id=1, source_target_pairs={{0,8},{8,16},{16,24},{24,0},{1,9},{9,17},{17,25},{25,1},{2,10},{10... | collective-permute-start | bytes 1474568 | tf_op jit(solution)/shard_map/ppermute | solution.py:642
  9.4 26.2 %collective-permute-start.3 = (f32[10,96,128]{2,1,0:T(8,128)}, f32[10,96,128]{2,1,0:T(8,128)S(1)}, u32[]{:S(2)}, u32[]{:S(2)}) collective-permute-start(f32[10,96,128]{2,1,0:T(8,128)} %get-tuple-element.31.refs_0_), channel_id=1, source_target_pairs={{8,0},{16,8},{24,16},{0,24},{9,1},{17,9},{25,17},{1,25},{10,2},{18... | collective-permute-start | bytes 1474568 | tf_op jit(solution)/shard_map/ppermute | solution.py:643
  11.5 24.1 %all-to-all-start = ((f32[32,1,128]{2,1,0:T(1,128)}), f32[32,1,128]{2,1,0:T(1,128)S(1)}, u32[]{:S(2)}, u32[]{:S(2)}) async-start(f32[32,1,128]{2,1,0:T(1,128)} %get-tuple-element.29.refs_6_), calls=%async_computation | async-start | bytes 32768 | tf_op jit(solution)/shard_map/all_to_all | solution.py:655
  19.7 17.1 %collective-permute-start = (f32[2,96,128]{2,1,0:T(8,128)}, f32[2,96,128]{2,1,0:T(8,128)S(1)}, u32[]{:S(2)}, u32[]{:S(2)}) collective-permute-start(f32[2,96,128]{2,1,0:T(8,128)} %ends.1.refs_5_), channel_id=1, source_target_pairs={{0,1},{1,2},{2,3},{3,4},{4,5},{5,6},{6,7},{7,0},{8,9},{9,10},{10,1... | collective-permute-start | bytes 294920 | tf_op jit(solution)/shard_map/ppermute | solution.py:672
  20.0 16.9 %collective-permute-start.1 = (f32[2,96,128]{2,1,0:T(8,128)}, f32[2,96,128]{2,1,0:T(8,128)S(1)}, u32[]{:S(2)}, u32[]{:S(2)}) collective-permute-start(f32[2,96,128]{2,1,0:T(8,128)} %ends.1.refs_5_), channel_id=1, source_target_pairs={{1,0},{2,1},{3,2},{4,3},{5,4},{6,5},{7,6},{0,7},{9,8},{10,9},{11,1... | collective-permute-start | bytes 294920 | tf_op jit(solution)/shard_map/ppermute | solution.py:673
  41.5 15.3 %collective-permute-start.6 = (f32[4,96,128]{2,1,0:T(8,128)}, f32[4,96,128]{2,1,0:T(8,128)S(1)}, u32[]{:S(2)}, u32[]{:S(2)}) collective-permute-start(f32[4,96,128]{2,1,0:T(8,128)} %get-tuple-element.32.refs_5_.refs_1_), channel_id=1, source_target_pairs={{0,8},{8,16},{16,24},{24,0},{1,9},{9,17},{17,25},{25,1},{2,10},{10... | collective-permute-start | bytes 589832 | tf_op jit(solution)/shard_map/ppermute | solution.py:642
  42.1 18.8 %collective-permute-start.7 = (f32[4,96,128]{2,1,0:T(8,128)}, f32[4,96,128]{2,1,0:T(8,128)S(1)}, u32[]{:S(2)}, u32[]{:S(2)}) collective-permute-start(f32[4,96,128]{2,1,0:T(8,128)} %get-tuple-element.35.refs_4_.refs_0_), channel_id=1, source_target_pairs={{8,0},{16,8},{24,16},{0,24},{9,1},{17,9},{25,17},{1,25},{10,2},{18... | collective-permute-start | bytes 589832 | tf_op jit(solution)/shard_map/ppermute | solution.py:643
  45.3 32.4 %all-to-all-start.1 = ((f32[32,16,128]{2,1,0:T(8,128)}), f32[32,16,128]{2,1,0:T(8,128)S(1)}, u32[]{:S(2)}, u32[]{:S(2)}) async-start(f32[32,16,128]{2,1,0:T(8,128)} %bitcast), calls=%async_computation.1 | async-start | bytes 524288 | tf_op jit(solution)/shard_map/all_to_all | solution.py:684
  52.9 30.6 %collective-permute-start.8 = (f32[12,96,128]{2,1,0:T(8,128)}, f32[12,96,128]{2,1,0:T(8,128)S(1)}, u32[]{:S(2)}, u32[]{:S(2)}) collective-permute-start(f32[12,96,128]{2,1,0:T(8,128)} %get-tuple-element.40.refs_1_), channel_id=1, source_target_pairs={{0,8},{8,16},{16,24},{24,0},{1,9},{9,17},{17,25},{25,1},{2,10},{10... | collective-permute-start | bytes 1769480 | tf_op jit(solution)/shard_map/ppermute | solution.py:642
  54.7 29.7 %collective-permute-start.9 = (f32[12,96,128]{2,1,0:T(8,128)}, f32[12,96,128]{2,1,0:T(8,128)S(1)}, u32[]{:S(2)}, u32[]{:S(2)}) collective-permute-start(f32[12,96,128]{2,1,0:T(8,128)} %get-tuple-element.39.refs_0_), channel_id=1, source_target_pairs={{8,0},{16,8},{24,16},{0,24},{9,1},{17,9},{25,17},{1,25},{10,2},{18... | collective-permute-start | bytes 1769480 | tf_op jit(solution)/shard_map/ppermute | solution.py:643
  56.8 36.5 %collective-permute-start.4 = (f32[3,96,128]{2,1,0:T(8,128)}, f32[3,96,128]{2,1,0:T(8,128)S(1)}, u32[]{:S(2)}, u32[]{:S(2)}) collective-permute-start(f32[3,96,128]{2,1,0:T(8,128)} %get-tuple-element.34.refs_1_), channel_id=1, source_target_pairs={{0,8},{8,16},{16,24},{24,0},{1,9},{9,17},{17,25},{25,1},{2,10},{10... | collective-permute-start | bytes 442376 | tf_op jit(solution)/shard_map/ppermute | solution.py:642
  56.8 4.1 %copy-start.11 = (f32[4,96,128]{2,1,0:T(8,128)}, f32[4,96,128]{2,1,0:T(8,128)S(1)}, u32[]{:S(2)}) copy-start(f32[4,96,128]{2,1,0:T(8,128)S(1)} %collective-permute-done.6.refs_6_.refs_2_) | copy-start | bytes 589828
  56.8 9.3 %copy-start.1 = (f32[10,96,128]{2,1,0:T(8,128)S(1)}, f32[10,96,128]{2,1,0:T(8,128)}, u32[]{:S(2)}) copy-start(f32[10,96,128]{2,1,0:T(8,128)} %get-tuple-element.30.refs_4_.refs_2_.refs_1_) | copy-start | bytes 1474564
  56.8 9.3 %copy-start.5 = (f32[10,96,128]{2,1,0:T(8,128)S(1)}, f32[10,96,128]{2,1,0:T(8,128)}, u32[]{:S(2)}) copy-start(f32[10,96,128]{2,1,0:T(8,128)} %get-tuple-element.31.refs_0_) | copy-start | bytes 1474564
  56.8 9.3 %copy-start.7 = (f32[10,96,128]{2,1,0:T(8,128)S(1)}, f32[10,96,128]{2,1,0:T(8,128)}, u32[]{:S(2)}) copy-start(f32[10,96,128]{2,1,0:T(8,128)} %copy-done.6) | copy-start | bytes 1474564
  56.8 9.3 %copy-start.9 = (f32[10,96,128]{2,1,0:T(8,128)S(1)}, f32[10,96,128]{2,1,0:T(8,128)}, u32[]{:S(2)}) copy-start(f32[10,96,128]{2,1,0:T(8,128)} %copy-done.8) | copy-start | bytes 1474564
  56.9 36.4 %collective-permute-start.5 = (f32[3,96,128]{2,1,0:T(8,128)}, f32[3,96,128]{2,1,0:T(8,128)}, u32[]{:S(2)}, u32[]{:S(2)}) collective-permute-start(f32[3,96,128]{2,1,0:T(8,128)} %get-tuple-element.33.refs_0_), channel_id=1, source_target_pairs={{8,0},{16,8},{24,16},{0,24},{9,1},{17,9},{25,17},{1,25},{10,2},{18... | collective-permute-start | bytes 442376 | tf_op jit(solution)/shard_map/ppermute | solution.py:643
  70.6 5.1 %copy-start.2 = (f32[4,96,128]{2,1,0:T(8,128)S(1)}, f32[4,96,128]{2,1,0:T(8,128)}, u32[]{:S(2)}) copy-start(f32[4,96,128]{2,1,0:T(8,128)} %get-tuple-element.32.refs_5_.refs_1_) | copy-start | bytes 589828
  70.6 5.1 %copy-start.10 = (f32[4,96,128]{2,1,0:T(8,128)S(1)}, f32[4,96,128]{2,1,0:T(8,128)}, u32[]{:S(2)}) copy-start(f32[4,96,128]{2,1,0:T(8,128)} %get-tuple-element.35.refs_4_.refs_0_) | copy-start | bytes 589828
  70.6 5.1 %copy-start.12 = (f32[4,96,128]{2,1,0:T(8,128)S(1)}, f32[4,96,128]{2,1,0:T(8,128)}, u32[]{:S(2)}) copy-start(f32[4,96,128]{2,1,0:T(8,128)} %copy-done.11) | copy-start | bytes 589828
  70.6 5.1 %copy-start.14 = (f32[4,96,128]{2,1,0:T(8,128)S(1)}, f32[4,96,128]{2,1,0:T(8,128)}, u32[]{:S(2)}) copy-start(f32[4,96,128]{2,1,0:T(8,128)} %copy-done.13) | copy-start | bytes 589828
  75.7 2.1 %copy-start.18 = (s32[2,128]{1,0:T(2,128)S(1)}, s32[2,128]{1,0:T(2,128)}, u32[]{:S(2)}) copy-start(s32[2,128]{1,0:T(2,128)} %refs_4_.4) | copy-start | bytes 3076
  75.7 2.1 %copy-start.27 = (s32[1,256]{1,0:T(1,128)S(1)}, s32[1,256]{1,0:T(1,128)}, u32[]{:S(2)}) copy-start(s32[1,256]{1,0:T(1,128)} %get-tuple-element.46.refs_2_) | copy-start | bytes 3076
  78.8 5.6 %copy-start.3 = (f32[12,96,128]{2,1,0:T(8,128)S(1)}, f32[12,96,128]{2,1,0:T(8,128)}, u32[]{:S(2)}) copy-start(f32[12,96,128]{2,1,0:T(8,128)} %get-tuple-element.40.refs_1_) | copy-start | bytes 1769476
  78.8 5.6 %copy-start.4 = (f32[12,96,128]{2,1,0:T(8,128)S(1)}, f32[12,96,128]{2,1,0:T(8,128)}, u32[]{:S(2)}) copy-start(f32[12,96,128]{2,1,0:T(8,128)} %get-tuple-element.39.refs_0_) | copy-start | bytes 1769476
  78.8 5.6 %copy-start.20 = (bf16[384,512]{1,0:T(8,128)(2,1)S(1)}, bf16[384,512]{1,0:T(8,128)(2,1)}, u32[]{:S(2)}) copy-start(bf16[384,512]{1,0:T(8,128)(2,1)} %constant.7.clone.refs_7_) | copy-start | bytes 1179652
  78.8 5.6 %copy-start.26 = (f32[2,96,128]{2,1,0:T(8,128)S(1)}, f32[2,96,128]{2,1,0:T(8,128)}, u32[]{:S(2)}) copy-start(f32[2,96,128]{2,1,0:T(8,128)} %get-tuple-element.38.refs_6_) | copy-start | bytes 294916
  80.6 15.7 %all-to-all-start.2 = ((f32[32,16,128]{2,1,0:T(8,128)}), f32[32,16,128]{2,1,0:T(8,128)S(1)}, u32[]{:S(2)}, u32[]{:S(2)}) async-start(f32[32,16,128]{2,1,0:T(8,128)} %bitcast.2), calls=%async_computation.2 | async-start | bytes 524288 | tf_op jit(solution)/shard_map/all_to_all | solution.py:763
  86.9 6.3 %copy-start.15 = (f32[3,96,128]{2,1,0:T(8,128)S(1)}, f32[3,96,128]{2,1,0:T(8,128)}, u32[]{:S(2)}) copy-start(f32[3,96,128]{2,1,0:T(8,128)} %get-tuple-element.34.refs_1_) | copy-start | bytes 442372
  86.9 6.4 %copy-start.16 = (f32[3,96,128]{2,1,0:T(8,128)S(1)}, f32[3,96,128]{2,1,0:T(8,128)}, u32[]{:S(2)}) copy-start(f32[3,96,128]{2,1,0:T(8,128)} %get-tuple-element.33.refs_0_) | copy-start | bytes 442372
  (14 other events, 15.3 us)

commit v3 on v2

--- a/solution.py
+++ b/solution.py
@@ -24,7 +24,7 @@
 HALF = LANES // 2
 PART = LANES // NP
 TYPES = NP - 1
-CHUNKS = (3, 1, 4, 1)
+CHUNKS = (3, 1, 3, 2)
 PARAMS = 6
 VM = pl.BlockSpec(memory_space=pltpu.VMEM)
 ANY = pl.BlockSpec(memory_space=pl.ANY)
@@ -654,7 +654,7 @@
     )(owner)
     counts_in = lax.all_to_all(counts, axes, split_axis=0, concat_axis=0, tiled=True)
 
-    send([0], 1, (mw, counts), [VM, ANY], "first_pack")
+    send([0], 1, (mw,), [VM], "first_pack")
 
     edges = pl.pallas_call(
         lambda *refs: ends_kernel(levels, ndyn, ntrc, *refs),

time: 98.3 us -> 96.8 us (0.985)
    all_to_all x1, waiting for transfers between devices: 0.01 us -> 1.51 us  [local(): lax.all_to_all(next_out, axes, split_axis=0, concat_axis=0, tiled=True)]
    all_to_all x1, waiting for transfers between devices: 13.2 us -> 11.7 us  [local(): lax.all_to_all(counts, axes, split_axis=0, concat_axis=0, tiled=True)]
    unnamed x66 -> x64, local copies, waits for them, and re-layouts: 10.7 us -> 10 us
  transfers between devices with their start and end apart: 13 -> 13, of which waited for: 2 -> 2; matrix products, arithmetic and copies ran while one was open for 0% -> 0% of each run, Pallas kernels for 33% -> 35%
where the time goes in v3:
time: 96.8 us; the launch traced here: 96 us
  Pallas kernels  42 us (43%)
  starting transfers between devices  29.6 us (31%)
  waiting for transfers between devices  13.3 us (14%)
  local copies, waits for them, and re-layouts  10 us (10%)
  between operations  1.05 us (1%)
    pallas_call x4, Pallas kernels, remap(): pl.pallas_call(lambda *refs: remap_kernel(levels, ndyn, chunk, aliased, l...  15.4 us
    pallas_call x3, Pallas kernels, send(): pl.pallas_call(lambda *refs: pack_kernel(levels, parts, numbers[0] == 0,...  12.5 us
    all_to_all x1, waiting for transfers between devices, local(): lax.all_to_all(counts, axes, split_axis=0, concat_axis=0, tiled=True)  11.7 us
    ppermute x4, starting transfers between devices, send(): lax.ppermute(sent[2 * i + 1], 'gx', down)  11.5 us
    unnamed x64, local copies, waits for them, and re-layouts  10 us
    ppermute x4, starting transfers between devices, send(): lax.ppermute(sent[2 * i], 'gx', up)  5.43 us
    pallas_call x1, Pallas kernels, local(): pl.pallas_call(lambda *refs: setup_kernel(levels, nfields, *refs), grid=(...  4.5 us
    all_to_all x1, starting transfers between devices, local(): lax.all_to_all(counts, axes, split_axis=0, concat_axis=0, tiled=True)  4.21 us
  transfers between devices with their start and end apart: 13, of which 2 were waited for; matrix products, arithmetic and copies ran while one was open for 0% of the time, Pallas kernels for 35%

profile of v3, /device:TPU:0, one launch (start us, length us, event | category | flops | bytes accessed | tf_op | source)
XLA Modules:
  0.0 96.0 jit_solution(12062018278899771862)
XLA Ops:
  0.6 4.3 %first_pack.1 = (f32[10,96,128]{2,1,0:T(8,128)}, f32[10,96,128]{2,1,0:T(8,128)}) custom-call(f32[3,93,2,128]{3,2,1,0:T(2,128)} %refs_0_.9, f32[33,93,2,128]{3,2,1,0:T(2,128)} %refs_1_.9, f32[93,2,128]{2,1,0:T(2,128)} %refs_2_.7, f32[2,128]{1,0:T(2,128)} %refs_3_.7, bf16[512,384]{1,0:T(8,128)(2,1)} %constant.6.clone.refs_4_, ...), custom_call_target="tpu_custom_call" | custom-call | flops 10000000 | bytes 30000 | tf_op jit(solution)/shard_map/first_pack/pallas_call | solution.py:624
  4.9 3.1 %collective-permute-start.2 = (f32[10,96,128]{2,1,0:T(8,128)}, f32[10,96,128]{2,1,0:T(8,128)S(1)}, u32[]{:S(2)}, u32[]{:S(2)}) collective-permute-start(f32[10,96,128]{2,1,0:T(8,128)} %get-tuple-element.29.refs_4_.refs_2_.refs_1_), channel_id=1, source_target_pairs={{0,8},{8,16},{16,24},{24,0},{1,9},{9,17},{17,25},{25,1},{2,10},{10... | collective-permute-start | bytes 1474568 | tf_op jit(solution)/shard_map/ppermute | solution.py:642
  8.0 2.1 %collective-permute-start.3 = (f32[10,96,128]{2,1,0:T(8,128)}, f32[10,96,128]{2,1,0:T(8,128)S(1)}, u32[]{:S(2)}, u32[]{:S(2)}) collective-permute-start(f32[10,96,128]{2,1,0:T(8,128)} %get-tuple-element.31.refs_0_), channel_id=1, source_target_pairs={{8,0},{16,8},{24,16},{0,24},{9,1},{17,9},{25,17},{1,25},{10,2},{18... | collective-permute-start | bytes 1474568 | tf_op jit(solution)/shard_map/ppermute | solution.py:643
  10.1 1.4 %route.1 = (f32[32,1,128]{2,1,0:T(1,128)}, s32[1,256]{1,0:T(1,128)}) custom-call(s32[2,128]{1,0:T(2,128)} %refs_0_.7), custom_call_target="tpu_custom_call" | custom-call | flops 10000000 | bytes 30000 | tf_op jit(solution)/shard_map/route/pallas_call | solution.py:646
  11.5 4.2 %all-to-all-start = ((f32[32,1,128]{2,1,0:T(1,128)}), f32[32,1,128]{2,1,0:T(1,128)S(1)}, u32[]{:S(2)}, u32[]{:S(2)}) async-start(f32[32,1,128]{2,1,0:T(1,128)} %get-tuple-element.30), calls=%async_computation | async-start | bytes 32768 | tf_op jit(solution)/shard_map/all_to_all | solution.py:655
  15.7 4.0 %ends.1.refs_5_ = f32[2,96,128]{2,1,0:T(8,128)} custom-call(f32[3,93,2,128]{3,2,1,0:T(2,128)} %refs_0_.9, f32[33,93,2,128]{3,2,1,0:T(2,128)} %refs_1_.9, f32[93,2,128]{2,1,0:T(2,128)} %refs_2_.7, f32[2,128]{1,0:T(2,128)} %refs_3_.7, f32[10,96,128]{2,1,0:T(8,128)} %get-tuple-element.29.refs_4_.refs_2_.refs_1_), custom_call_target="tpu_custom_call" | custom-call | flops 10000000 | bytes 30000 | tf_op jit(solution)/shard_map/ends/pallas_call | solution.py:659
  20.0 2.4 %collective-permute-start.1 = (f32[2,96,128]{2,1,0:T(8,128)}, f32[2,96,128]{2,1,0:T(8,128)S(1)}, u32[]{:S(2)}, u32[]{:S(2)}) collective-permute-start(f32[2,96,128]{2,1,0:T(8,128)} %ends.1.refs_5_), channel_id=1, source_target_pairs={{1,0},{2,1},{3,2},{4,3},{5,4},{6,5},{7,6},{0,7},{9,8},{10,9},{11,1... | collective-permute-start | bytes 294920 | tf_op jit(solution)/shard_map/ppermute | solution.py:673
  22.4 11.7 %all-to-all-done.refs_0_ = f32[32,1,128]{2,1,0:T(1,128)S(1)} async-done(((f32[32,1,128]{2,1,0:T(1,128)}), f32[32,1,128]{2,1,0:T(1,128)S(1)}, u32[]{:S(2)}, u32[]{:S(2)}) %all-to-all-start) | async-done | bytes 16416 | tf_op jit(solution)/shard_map/all_to_all | solution.py:655
  34.2 1.2 %cloud_send.1.refs_8_ = f32[512,128]{1,0:T(8,128)} custom-call(f32[32,1,128]{2,1,0:T(1,128)S(1)} %all-to-all-done.refs_0_, f32[93,256]{1,0:T(8,128)S(1)} %copy-done.15, f32[10,96,128]{2,1,0:T(8,128)S(1)} %copy-done, f32[10,96,128]{2,1,0:T(8,128)S(1)} %collective-permute-done.2.refs_3_.refs_2_, f32[10,96,128]{2,1,0:T(8,128)S(1)} %collective-permute-done.3.refs_4_.refs_3_), custom_call_target="tpu_custom_call" | custom-call | flops 2000000000 | bytes 6000000 | tf_op jit(solution)/shard_map/cloud_send/pallas_call | solution.py:675
  36.7 3.3 %second_pack.1 = (f32[4,96,128]{2,1,0:T(8,128)}, f32[4,96,128]{2,1,0:T(8,128)}) custom-call(f32[3,93,2,128]{3,2,1,0:T(2,128)} %refs_0_.9, f32[33,93,2,128]{3,2,1,0:T(2,128)} %refs_1_.9, f32[93,2,128]{2,1,0:T(2,128)} %refs_2_.7, f32[2,128]{1,0:T(2,128)} %refs_3_.7, bf16[512,384]{1,0:T(8,128)(2,1)} %constant.6.clone.refs_4_, f32[2,96,128]{2,1,0:T(8,128)} %ends.1.refs_5_, ...), custom_call_target="tpu_custom_call" | custom-call | flops 10000000 | bytes 30000 | tf_op jit(solution)/shard_map/second_pack/pallas_call | solution.py:624
  40.7 3.2 %collective-permute-start.7 = (f32[4,96,128]{2,1,0:T(8,128)}, f32[4,96,128]{2,1,0:T(8,128)}, u32[]{:S(2)}, u32[]{:S(2)}) collective-permute-start(f32[4,96,128]{2,1,0:T(8,128)} %get-tuple-element.35.refs_4_.refs_0_), channel_id=1, source_target_pairs={{8,0},{16,8},{24,16},{0,24},{9,1},{17,9},{25,17},{1,25},{10,2},{18... | collective-permute-start | bytes 589832 | tf_op jit(solution)/shard_map/ppermute | solution.py:643
  43.9 2.6 %all-to-all-start.1 = ((f32[32,16,128]{2,1,0:T(8,128)}), f32[32,16,128]{2,1,0:T(8,128)S(1)}, u32[]{:S(2)}, u32[]{:S(2)}) async-start(f32[32,16,128]{2,1,0:T(8,128)} %bitcast), calls=%async_computation.1 | async-start | bytes 524288 | tf_op jit(solution)/shard_map/all_to_all | solution.py:684
  46.5 5.0 %pack.1 = (f32[9,96,128]{2,1,0:T(8,128)}, f32[9,96,128]{2,1,0:T(8,128)}, f32[6,96,128]{2,1,0:T(8,128)}, f32[6,96,128]{2,1,0:T(8,128)}) custom-call(f32[3,93,2,128]{3,2,1,0:T(2,128)} %refs_0_.9, f32[33,93,2,128]{3,2,1,0:T(2,128)} %refs_1_.9, f32[93,2,128]{2,1,0:T(2,128)} %refs_2_.7, f32[2,128]{1,0:T(2,128)} %refs_3_.7, ...), custom_call_target="tpu_custom_call" | custom-call | flops 10000000 | bytes 30000 | tf_op jit(solution)/shard_map/pack/pallas_call | solution.py:624
  51.5 1.7 %collective-permute-start.8 = (f32[9,96,128]{2,1,0:T(8,128)}, f32[9,96,128]{2,1,0:T(8,128)S(1)}, u32[]{:S(2)}, u32[]{:S(2)}) collective-permute-start(f32[9,96,128]{2,1,0:T(8,128)} %get-tuple-element.40.refs_1_), channel_id=1, source_target_pairs={{0,8},{8,16},{16,24},{24,0},{1,9},{9,17},{17,25},{25,1},{2,10},{10... | collective-permute-start | bytes 1327112 | tf_op jit(solution)/shard_map/ppermute | solution.py:642
  53.2 2.1 %collective-permute-start.9 = (f32[9,96,128]{2,1,0:T(8,128)}, f32[9,96,128]{2,1,0:T(8,128)S(1)}, u32[]{:S(2)}, u32[]{:S(2)}) collective-permute-start(f32[9,96,128]{2,1,0:T(8,128)} %get-tuple-element.39.refs_0_), channel_id=1, source_target_pairs={{8,0},{16,8},{24,16},{0,24},{9,1},{17,9},{25,17},{1,25},{10,2},{18... | collective-permute-start | bytes 1327112 | tf_op jit(solution)/shard_map/ppermute | solution.py:643
  55.4 4.0 %collective-permute-start.5 = (f32[6,96,128]{2,1,0:T(8,128)}, f32[6,96,128]{2,1,0:T(8,128)S(1)}, u32[]{:S(2)}, u32[]{:S(2)}) collective-permute-start(f32[6,96,128]{2,1,0:T(8,128)} %get-tuple-element.33.refs_0_), channel_id=1, source_target_pairs={{8,0},{16,8},{24,16},{0,24},{9,1},{17,9},{25,17},{1,25},{10,2},{18... | collective-permute-start | bytes 884744 | tf_op jit(solution)/shard_map/ppermute | solution.py:643
  59.5 4.5 %column_setup.1 = (f32[6,6,96,128]{3,2,1,0:T(8,128)}, s32[6,2,96,128]{3,2,1,0:T(8,128)}, f32[2,96,128]{2,1,0:T(8,128)}, f32[1,256]{1,0:T(1,128)}) custom-call(f32[10,96,128]{2,1,0:T(8,128)} %get-tuple-element.31.refs_0_, f32[10,96,128]{2,1,0:T(8,128)} %get-tuple-element.29.refs_4_.refs_2_.refs_1_, f32[10,96,128]{2,1,0:T(8,128)} %copy-done.4, ...), custom_call_target="tpu_custom_call" | custom-call | flops 5000000000 | bytes 15000000 | tf_op jit(solution)/shard_map/column_setup/pallas_call | solution.py:696
  64.0 1.0 %copy-done.17 = bf16[384,512]{1,0:T(8,128)(2,1)S(1)} copy-done((bf16[384,512]{1,0:T(8,128)(2,1)S(1)}, bf16[384,512]{1,0:T(8,128)(2,1)}, u32[]{:S(2)}) %copy-start.17) | copy-done | bytes 393240
  65.0 1.5 %copy-done.19 = f32[6,6,96,128]{3,2,1,0:T(8,128)S(1)} copy-done((f32[6,6,96,128]{3,2,1,0:T(8,128)S(1)}, f32[6,6,96,128]{3,2,1,0:T(8,128)}, u32[]{:S(2)}) %copy-start.19) | copy-done | bytes 1769496
  66.5 1.1 %copy-done.22 = s32[6,2,96,128]{3,2,1,0:T(8,128)S(1)} copy-done((s32[6,2,96,128]{3,2,1,0:T(8,128)S(1)}, s32[6,2,96,128]{3,2,1,0:T(8,128)}, u32[]{:S(2)}) %copy-start.22) | copy-done | bytes 589848
  67.6 0.9 copy-done.24
  68.5 4.3 %remap.4 = (f32[3,93,2,128]{3,2,1,0:T(2,128)}, f32[33,93,2,128]{3,2,1,0:T(2,128)}, f32[4,96,256]{2,1,0:T(8,128)S(1)}) custom-call(f32[10,96,128]{2,1,0:T(8,128)S(1)} %copy-done.3, f32[10,96,128]{2,1,0:T(8,128)S(1)} %copy-done.1, f32[10,96,128]{2,1,0:T(8,128)S(1)} %copy-done.5, f32[10,96,128]{2,1,0:T(8,128)S(1)} %copy-done.7, ...), custom_call_target="tpu_custom_call" | custom-call | flops 6000000000 | bytes 18000000 | tf_op jit(solution)/shard_map/remap/pallas_call | solution.py:732
  73.6 3.0 %remap.5 = (f32[3,93,2,128]{3,2,1,0:T(2,128)}, f32[33,93,2,128]{3,2,1,0:T(2,128)}) custom-call(f32[4,96,128]{2,1,0:T(8,128)S(1)} %copy-done.12, f32[4,96,128]{2,1,0:T(8,128)S(1)} %copy-done.2, f32[4,96,128]{2,1,0:T(8,128)S(1)} %copy-done.14, f32[4,96,128]{2,1,0:T(8,128)} %collective-permute-done.7.refs_7_.refs_3_, ...), custom_call_target="tpu_custom_call", output_to_operand_aliasing={{0}: (8, {}), {1}: (9, {})} | custom-call | flops 2000000000 | bytes 6000000 | tf_op jit(solution)/shard_map/remap/pallas_call | solution.py:732
  76.6 1.0 %copy-done.28 = f32[4,96,256]{2,1,0:T(8,128)S(1)} copy-done((f32[4,96,256]{2,1,0:T(8,128)S(1)}, f32[4,96,256]{2,1,0:T(8,128)}, u32[]{:S(2)}) %copy-start.28) | copy-done | bytes 393240
  77.6 1.7 %physics.1 = (f32[4,93,2,128]{3,2,1,0:T(2,128)}, f32[512,128]{1,0:T(8,128)}) custom-call(f32[4,96,256]{2,1,0:T(8,128)S(1)} %copy-done.28, f32[512,128]{1,0:T(8,128)S(1)} %bitcast.4, s32[1,256]{1,0:T(1,128)S(1)} %copy-done.26, f32[1,256]{1,0:T(1,128)S(1)} %copy-done.29, s32[2,128]{1,0:T(2,128)S(1)} %copy-done.16), custom_call_target="tpu_custom_call" | custom-call | flops 5000000000 | bytes 15000000 | tf_op jit(solution)/shard_map/physics/pallas_call | solution.py:753
  79.3 3.2 %all-to-all-start.2 = ((f32[32,16,128]{2,1,0:T(8,128)}), f32[32,16,128]{2,1,0:T(8,128)S(1)}, u32[]{:S(2)}, u32[]{:S(2)}) async-start(f32[32,16,128]{2,1,0:T(8,128)} %bitcast.2), calls=%async_computation.2 | async-start | bytes 524288 | tf_op jit(solution)/shard_map/all_to_all | solution.py:763
  82.6 1.5 %copy-done.21 = f32[6,6,96,128]{3,2,1,0:T(8,128)S(1)} copy-done((f32[6,6,96,128]{3,2,1,0:T(8,128)S(1)}, f32[6,6,96,128]{3,2,1,0:T(8,128)}, u32[]{:S(2)}) %copy-start.21) | copy-done | bytes 1769496
  84.0 1.1 %copy-done.23 = s32[6,2,96,128]{3,2,1,0:T(8,128)S(1)} copy-done((s32[6,2,96,128]{3,2,1,0:T(8,128)S(1)}, s32[6,2,96,128]{3,2,1,0:T(8,128)}, u32[]{:S(2)}) %copy-start.23) | copy-done | bytes 589848
  85.1 4.9 %remap.6 = (f32[3,93,2,128]{3,2,1,0:T(2,128)}, f32[33,93,2,128]{3,2,1,0:T(2,128)}) custom-call(f32[9,96,128]{2,1,0:T(8,128)S(1)} %copy-done.9, f32[9,96,128]{2,1,0:T(8,128)S(1)} %copy-done.8, f32[9,96,128]{2,1,0:T(8,128)S(1)} %collective-permute-done.8.refs_2_, ...), custom_call_target="tpu_custom_call", output_to_operand_aliasing={{0}: (8, {}), {1}: (9, {})} | custom-call | flops 6000000000 | bytes 18000000 | tf_op jit(solution)/shard_map/remap/pallas_call | solution.py:732
  90.0 3.2 %remap.7 = (f32[3,93,2,128]{3,2,1,0:T(2,128)}, f32[33,93,2,128]{3,2,1,0:T(2,128)}) custom-call(f32[6,96,128]{2,1,0:T(8,128)S(1)} %copy-done.11, f32[6,96,128]{2,1,0:T(8,128)S(1)} %copy-done.10, f32[6,96,128]{2,1,0:T(8,128)S(1)} %collective-permute-done.4.refs_2_, ...), custom_call_target="tpu_custom_call", output_to_operand_aliasing={{0}: (8, {}), {1}: (9, {})} | custom-call | flops 4000000000 | bytes 12000000 | tf_op jit(solution)/shard_map/remap/pallas_call | solution.py:732
  93.2 1.5 %all-to-all-done.2 = f32[32,16,128]{2,1,0:T(8,128)S(1)} async-done(((f32[32,16,128]{2,1,0:T(8,128)}), f32[32,16,128]{2,1,0:T(8,128)S(1)}, u32[]{:S(2)}, u32[]{:S(2)}) %all-to-all-start.2) | async-done | bytes 262176 | tf_op jit(solution)/shard_map/all_to_all | solution.py:763
  94.8 1.2 %cloud_receive.1 = f32[93,256]{1,0:T(8,128)} custom-call(f32[32,1,128]{2,1,0:T(1,128)S(1)} %all-to-all-done.refs_0_, f32[512,128]{1,0:T(8,128)S(1)} %bitcast.5), custom_call_target="tpu_custom_call" | custom-call | flops 2000000000 | bytes 6000000 | tf_op jit(solution)/shard_map/cloud_receive/pallas_call | solution.py:769
  (71 shorter events, 3.1 us)
Async XLA Ops:
  0.6 33.6 %copy-start.15 = (f32[93,256]{1,0:T(8,128)S(1)}, f32[93,256]{1,0:T(8,128)}, u32[]{:S(2)}) copy-start(f32[93,256]{1,0:T(8,128)} %refs_1_.7) | copy-start | bytes 285700
  4.9 29.3 %copy-start = (f32[10,96,128]{2,1,0:T(8,128)S(1)}, f32[10,96,128]{2,1,0:T(8,128)}, u32[]{:S(2)}) copy-start(f32[10,96,128]{2,1,0:T(8,128)} %get-tuple-element.29.refs_4_.refs_2_.refs_1_) | copy-start | bytes 1474564
  4.9 29.2 %collective-permute-start.2 = (f32[10,96,128]{2,1,0:T(8,128)}, f32[10,96,128]{2,1,0:T(8,128)S(1)}, u32[]{:S(2)}, u32[]{:S(2)}) collective-permute-start(f32[10,96,128]{2,1,0:T(8,128)} %get-tuple-element.29.refs_4_.refs_2_.refs_1_), channel_id=1, source_target_pairs={{0,8},{8,16},{16,24},{24,0},{1,9},{9,17},{17,25},{25,1},{2,10},{10... | collective-permute-start | bytes 1474568 | tf_op jit(solution)/shard_map/ppermute | solution.py:642
  8.0 26.2 %collective-permute-start.3 = (f32[10,96,128]{2,1,0:T(8,128)}, f32[10,96,128]{2,1,0:T(8,128)S(1)}, u32[]{:S(2)}, u32[]{:S(2)}) collective-permute-start(f32[10,96,128]{2,1,0:T(8,128)} %get-tuple-element.31.refs_0_), channel_id=1, source_target_pairs={{8,0},{16,8},{24,16},{0,24},{9,1},{17,9},{25,17},{1,25},{10,2},{18... | collective-permute-start | bytes 1474568 | tf_op jit(solution)/shard_map/ppermute | solution.py:643
  11.5 22.6 %all-to-all-start = ((f32[32,1,128]{2,1,0:T(1,128)}), f32[32,1,128]{2,1,0:T(1,128)S(1)}, u32[]{:S(2)}, u32[]{:S(2)}) async-start(f32[32,1,128]{2,1,0:T(1,128)} %get-tuple-element.30), calls=%async_computation | async-start | bytes 32768 | tf_op jit(solution)/shard_map/all_to_all | solution.py:655
  19.7 15.7 %collective-permute-start = (f32[2,96,128]{2,1,0:T(8,128)}, f32[2,96,128]{2,1,0:T(8,128)S(1)}, u32[]{:S(2)}, u32[]{:S(2)}) collective-permute-start(f32[2,96,128]{2,1,0:T(8,128)} %ends.1.refs_5_), channel_id=1, source_target_pairs={{0,1},{1,2},{2,3},{3,4},{4,5},{5,6},{6,7},{7,0},{8,9},{9,10},{10,1... | collective-permute-start | bytes 294920 | tf_op jit(solution)/shard_map/ppermute | solution.py:672
  20.0 15.4 %collective-permute-start.1 = (f32[2,96,128]{2,1,0:T(8,128)}, f32[2,96,128]{2,1,0:T(8,128)S(1)}, u32[]{:S(2)}, u32[]{:S(2)}) collective-permute-start(f32[2,96,128]{2,1,0:T(8,128)} %ends.1.refs_5_), channel_id=1, source_target_pairs={{1,0},{2,1},{3,2},{4,3},{5,4},{6,5},{7,6},{0,7},{9,8},{10,9},{11,1... | collective-permute-start | bytes 294920 | tf_op jit(solution)/shard_map/ppermute | solution.py:673
  40.0 15.4 %collective-permute-start.6 = (f32[4,96,128]{2,1,0:T(8,128)}, f32[4,96,128]{2,1,0:T(8,128)S(1)}, u32[]{:S(2)}, u32[]{:S(2)}) collective-permute-start(f32[4,96,128]{2,1,0:T(8,128)} %get-tuple-element.32.refs_5_.refs_1_), channel_id=1, source_target_pairs={{0,8},{8,16},{16,24},{24,0},{1,9},{9,17},{17,25},{25,1},{2,10},{10... | collective-permute-start | bytes 589832 | tf_op jit(solution)/shard_map/ppermute | solution.py:642
  40.7 18.8 %collective-permute-start.7 = (f32[4,96,128]{2,1,0:T(8,128)}, f32[4,96,128]{2,1,0:T(8,128)}, u32[]{:S(2)}, u32[]{:S(2)}) collective-permute-start(f32[4,96,128]{2,1,0:T(8,128)} %get-tuple-element.35.refs_4_.refs_0_), channel_id=1, source_target_pairs={{8,0},{16,8},{24,16},{0,24},{9,1},{17,9},{25,17},{1,25},{10,2},{18... | collective-permute-start | bytes 589832 | tf_op jit(solution)/shard_map/ppermute | solution.py:643
  43.9 32.6 %all-to-all-start.1 = ((f32[32,16,128]{2,1,0:T(8,128)}), f32[32,16,128]{2,1,0:T(8,128)S(1)}, u32[]{:S(2)}, u32[]{:S(2)}) async-start(f32[32,16,128]{2,1,0:T(8,128)} %bitcast), calls=%async_computation.1 | async-start | bytes 524288 | tf_op jit(solution)/shard_map/all_to_all | solution.py:684
  51.5 31.0 %collective-permute-start.8 = (f32[9,96,128]{2,1,0:T(8,128)}, f32[9,96,128]{2,1,0:T(8,128)S(1)}, u32[]{:S(2)}, u32[]{:S(2)}) collective-permute-start(f32[9,96,128]{2,1,0:T(8,128)} %get-tuple-element.40.refs_1_), channel_id=1, source_target_pairs={{0,8},{8,16},{16,24},{24,0},{1,9},{9,17},{17,25},{25,1},{2,10},{10... | collective-permute-start | bytes 1327112 | tf_op jit(solution)/shard_map/ppermute | solution.py:642
  53.2 29.3 %collective-permute-start.9 = (f32[9,96,128]{2,1,0:T(8,128)}, f32[9,96,128]{2,1,0:T(8,128)S(1)}, u32[]{:S(2)}, u32[]{:S(2)}) collective-permute-start(f32[9,96,128]{2,1,0:T(8,128)} %get-tuple-element.39.refs_0_), channel_id=1, source_target_pairs={{8,0},{16,8},{24,16},{0,24},{9,1},{17,9},{25,17},{1,25},{10,2},{18... | collective-permute-start | bytes 1327112 | tf_op jit(solution)/shard_map/ppermute | solution.py:643
  55.4 34.6 %collective-permute-start.4 = (f32[6,96,128]{2,1,0:T(8,128)}, f32[6,96,128]{2,1,0:T(8,128)S(1)}, u32[]{:S(2)}, u32[]{:S(2)}) collective-permute-start(f32[6,96,128]{2,1,0:T(8,128)} %get-tuple-element.34.refs_1_), channel_id=1, source_target_pairs={{0,8},{8,16},{16,24},{24,0},{1,9},{9,17},{17,25},{25,1},{2,10},{10... | collective-permute-start | bytes 884744 | tf_op jit(solution)/shard_map/ppermute | solution.py:642
  55.4 4.1 %copy-start.13 = (f32[4,96,128]{2,1,0:T(8,128)}, f32[4,96,128]{2,1,0:T(8,128)S(1)}, u32[]{:S(2)}) copy-start(f32[4,96,128]{2,1,0:T(8,128)S(1)} %collective-permute-done.6.refs_6_.refs_2_) | copy-start | bytes 589828
  55.4 8.6 %copy-start.1 = (f32[10,96,128]{2,1,0:T(8,128)S(1)}, f32[10,96,128]{2,1,0:T(8,128)}, u32[]{:S(2)}) copy-start(f32[10,96,128]{2,1,0:T(8,128)} %get-tuple-element.29.refs_4_.refs_2_.refs_1_) | copy-start | bytes 1474564
  55.4 8.6 %copy-start.3 = (f32[10,96,128]{2,1,0:T(8,128)S(1)}, f32[10,96,128]{2,1,0:T(8,128)}, u32[]{:S(2)}) copy-start(f32[10,96,128]{2,1,0:T(8,128)} %get-tuple-element.31.refs_0_) | copy-start | bytes 1474564
  55.4 8.6 %copy-start.5 = (f32[10,96,128]{2,1,0:T(8,128)S(1)}, f32[10,96,128]{2,1,0:T(8,128)}, u32[]{:S(2)}) copy-start(f32[10,96,128]{2,1,0:T(8,128)} %copy-done.4) | copy-start | bytes 1474564
  55.4 8.6 %copy-start.7 = (f32[10,96,128]{2,1,0:T(8,128)S(1)}, f32[10,96,128]{2,1,0:T(8,128)}, u32[]{:S(2)}) copy-start(f32[10,96,128]{2,1,0:T(8,128)} %copy-done.6) | copy-start | bytes 1474564
  55.4 34.6 %collective-permute-start.5 = (f32[6,96,128]{2,1,0:T(8,128)}, f32[6,96,128]{2,1,0:T(8,128)S(1)}, u32[]{:S(2)}, u32[]{:S(2)}) collective-permute-start(f32[6,96,128]{2,1,0:T(8,128)} %get-tuple-element.33.refs_0_), channel_id=1, source_target_pairs={{8,0},{16,8},{24,16},{0,24},{9,1},{17,9},{25,17},{1,25},{10,2},{18... | collective-permute-start | bytes 884744 | tf_op jit(solution)/shard_map/ppermute | solution.py:643
  68.5 5.1 %copy-start.2 = (f32[4,96,128]{2,1,0:T(8,128)S(1)}, f32[4,96,128]{2,1,0:T(8,128)}, u32[]{:S(2)}) copy-start(f32[4,96,128]{2,1,0:T(8,128)} %get-tuple-element.32.refs_5_.refs_1_) | copy-start | bytes 589828
  68.5 5.1 %copy-start.12 = (f32[4,96,128]{2,1,0:T(8,128)S(1)}, f32[4,96,128]{2,1,0:T(8,128)}, u32[]{:S(2)}) copy-start(f32[4,96,128]{2,1,0:T(8,128)} %get-tuple-element.35.refs_4_.refs_0_) | copy-start | bytes 589828
  68.5 5.1 %copy-start.14 = (f32[4,96,128]{2,1,0:T(8,128)S(1)}, f32[4,96,128]{2,1,0:T(8,128)}, u32[]{:S(2)}) copy-start(f32[4,96,128]{2,1,0:T(8,128)} %copy-done.13) | copy-start | bytes 589828
  68.5 5.1 %copy-start.20 = (f32[6,6,96,128]{3,2,1,0:T(8,128)S(1)}, f32[6,6,96,128]{3,2,1,0:T(8,128)}, u32[]{:S(2)}) copy-start(f32[6,6,96,128]{3,2,1,0:T(8,128)} %get-tuple-element.36.refs_4_) | copy-start | bytes 5308420
  68.5 5.1 %copy-start.25 = (f32[2,96,128]{2,1,0:T(8,128)S(1)}, f32[2,96,128]{2,1,0:T(8,128)}, u32[]{:S(2)}) copy-start(f32[2,96,128]{2,1,0:T(8,128)} %get-tuple-element.38.refs_6_) | copy-start | bytes 294916
  73.5 3.0 %copy-start.16 = (s32[2,128]{1,0:T(2,128)S(1)}, s32[2,128]{1,0:T(2,128)}, u32[]{:S(2)}) copy-start(s32[2,128]{1,0:T(2,128)} %refs_4_.4) | copy-start | bytes 3076
  73.5 3.0 %copy-start.26 = (s32[1,256]{1,0:T(1,128)S(1)}, s32[1,256]{1,0:T(1,128)}, u32[]{:S(2)}) copy-start(s32[1,256]{1,0:T(1,128)} %get-tuple-element.46.refs_2_) | copy-start | bytes 3076
  77.6 4.9 %copy-start.8 = (f32[9,96,128]{2,1,0:T(8,128)S(1)}, f32[9,96,128]{2,1,0:T(8,128)}, u32[]{:S(2)}) copy-start(f32[9,96,128]{2,1,0:T(8,128)} %get-tuple-element.40.refs_1_) | copy-start | bytes 1327108
  77.6 4.9 %copy-start.9 = (f32[9,96,128]{2,1,0:T(8,128)S(1)}, f32[9,96,128]{2,1,0:T(8,128)}, u32[]{:S(2)}) copy-start(f32[9,96,128]{2,1,0:T(8,128)} %get-tuple-element.39.refs_0_) | copy-start | bytes 1327108
  77.6 4.9 %copy-start.18 = (bf16[384,512]{1,0:T(8,128)(2,1)S(1)}, bf16[384,512]{1,0:T(8,128)(2,1)}, u32[]{:S(2)}) copy-start(bf16[384,512]{1,0:T(8,128)(2,1)} %constant.7.clone.refs_7_) | copy-start | bytes 1179652
  79.3 15.4 %all-to-all-start.2 = ((f32[32,16,128]{2,1,0:T(8,128)}), f32[32,16,128]{2,1,0:T(8,128)S(1)}, u32[]{:S(2)}, u32[]{:S(2)}) async-start(f32[32,16,128]{2,1,0:T(8,128)} %bitcast.2), calls=%async_computation.2 | async-start | bytes 524288 | tf_op jit(solution)/shard_map/all_to_all | solution.py:763
  85.1 4.9 %copy-start.10 = (f32[6,96,128]{2,1,0:T(8,128)S(1)}, f32[6,96,128]{2,1,0:T(8,128)}, u32[]{:S(2)}) copy-start(f32[6,96,128]{2,1,0:T(8,128)} %get-tuple-element.34.refs_1_) | copy-start | bytes 884740
  85.1 4.9 %copy-start.11 = (f32[6,96,128]{2,1,0:T(8,128)S(1)}, f32[6,96,128]{2,1,0:T(8,128)}, u32[]{:S(2)}) copy-start(f32[6,96,128]{2,1,0:T(8,128)} %get-tuple-element.33.refs_0_) | copy-start | bytes 884740
  (13 other events, 15.5 us)
